TPU v7x, 256 devices: a whole 4x4x8 slice. The times are simulated.
256 devices in a mesh: pipe: 32 (over z_lo, x, core), tensor: 8 (over y, z_hi).
Axes of the slice: x: 4, y: 4, z: 8 (z_hi: 2, z_lo: 4; z = z_hi * 4 + z_lo), core: 2. Of those that a mesh axis runs over, the one named last changes fastest.
Arguments:
- down_prev: bfloat16 [32, 256, 4096], P('pipe', 'tensor'), may hold values from -6 to 6
- up_prev: bfloat16 [32, 256, 4096], P('pipe', 'tensor'), may hold values from -6 to 6
- down_stash: bfloat16 [32, 256, 4096], P('pipe', 'tensor'), may hold values from -6 to 6
- up_stash: bfloat16 [32, 256, 4096], P('pipe', 'tensor'), may hold values from -6 to 6
- down_cot: bfloat16 [32, 256, 4096], P('pipe', 'tensor'), may hold values from -0.75 to 0.75
- up_cot: bfloat16 [32, 256, 4096], P('pipe', 'tensor'), may hold values from -0.75 to 0.75
- boundary: bfloat16 [4, 256, 4096], P(None, 'tensor'), may hold values from -3 to 3
- segment_ids: int32 [4, 32, 256], P(None, 'pipe'), may hold values from 0 to 31, never falling along the last dimension, each value on 1 to 128 neighbouring positions
- value_weight: bfloat16 [32, 2, 4096, 1024], P('pipe', None, None, 'tensor'), as said below
- output_weight: bfloat16 [32, 2, 1024, 4096], P('pipe', None, 'tensor'), as said below
Outputs:
- down_out: bfloat16 [32, 256, 4096], P('pipe', 'tensor')
- up_out: bfloat16 [32, 256, 4096], P('pipe', 'tensor')
- down_back: bfloat16 [32, 256, 4096], P('pipe', 'tensor')
- up_back: bfloat16 [32, 256, 4096], P('pipe', 'tensor')
- value_grad: float32 [32, 4096, 1024], P('pipe', None, 'tensor')
- output_grad: float32 [32, 1024, 4096], P('pipe', 'tensor')
Inputs may be any that keep to these rules, and one draw needn't show every extreme that they name: `segment_ids`: ids never fall along a micro-batch's tokens. `value_weight`: entry [r, 1] equals entry [31 - r, 0]: both copies of a section are equal. `output_weight`: entry [r, 1] equals entry [31 - r, 0]: both copies of a section are equal.
All inputs are finite; a program needn't handle non-finite values.
Results may differ from a plain program's by a relative error of at most 0.012.
Values may be sent and summed in bfloat16 or wider, within the bound.
No kernel may reach another device: no remote copies, remote signals or barrier semaphores. Data moves between devices by JAX's collectives and lax.ppermute only.
A program may use at most 128 MiB of HBM per device.

v0:
```python
import jax
import jax.numpy as jnp
from jax import lax
from jax.sharding import PartitionSpec as P

eps = 1e-05

RANKS = 32
LANES = 8
RING = 4
ROWS = 32


def spot(rank, row, half):
    return (rank % RANKS) * LANES + (row % RING) * 2 + half % 2


def moved(shard, rank_to, half_by=0):
    pairs = [
        (spot(r, y, z), spot(rank_to(r), y, z + half_by))
        for r in range(RANKS)
        for y in range(RING)
        for z in range(2)
    ]
    return lax.ppermute(shard, ("pipe", "tensor"), pairs)


def stay(r):
    return r


def up_one(r):
    return r + 1


def down_one(r):
    return r - 1


def mirror(r):
    return RANKS - 1 - r


def mirror_next(r):
    return RANKS - 2 - r


def mirror_prev(r):
    return RANKS - r


def turned(blocks):
    return lax.all_to_all(
        blocks,
        "tensor",
        split_axis=0,
        concat_axis=0,
        axis_index_groups=[[0, 2, 4, 6], [1, 3, 5, 7]],
        tiled=True,
    )


def shared(block):
    return turned(jnp.broadcast_to(block[None], (RING,) + block.shape))


def columns_out(rows):
    k, n, d = rows.shape
    return turned(rows.reshape(k, n, RING, d // RING).transpose(2, 0, 1, 3))


def columns_back(blocks):
    back = turned(blocks)
    q, k, n, c = back.shape
    return back.transpose(1, 2, 0, 3).reshape(k, n, q * c)


def normalize(inputs):
    widened = inputs.astype(jnp.float32)
    inverse_rms = lax.rsqrt(jnp.mean(widened * widened, axis=-1, keepdims=True) + eps)
    return (widened * inverse_rms, inverse_rms)


def product(spec, left, right):
    return jnp.einsum(spec, left, right, preferred_element_type=jnp.float32)


def token_order():
    half = lax.axis_index("tensor") % 2
    halves = jnp.stack([half, 1 - half])
    rows = jnp.arange(RING, dtype=jnp.int32)
    within = jnp.arange(ROWS, dtype=jnp.int32)
    lanes = rows[None, :] * 2 + halves[:, None]
    return (lanes[:, :, None] * ROWS + within[None, None, :]).reshape(-1)


def segment_mask(segment_row, order):
    by_half = segment_row.reshape(RING, 2, ROWS).transpose(1, 0, 2)
    half = lax.axis_index("tensor") % 2
    segments = jnp.where(half == 0, by_half, by_half[::-1]).reshape(-1)
    causal = order[:, None] >= order[None, :]
    same_segment = segments[:, None] == segments[None, :]
    allowed = jnp.logical_and(causal, same_segment)
    return (
        allowed.astype(jnp.bfloat16),
        jnp.sum(allowed.astype(jnp.float32), axis=1, keepdims=True),
    )


def summed_over_ring(parts):
    return jnp.sum(turned(parts.astype(jnp.bfloat16)).astype(jnp.float32), axis=0)


def mixed_of(normed, masks, value_cols):
    values = summed_over_ring(product("rd,hdk->hrk", normed, value_cols)).astype(jnp.bfloat16)
    tokens = values.shape[0] // 2
    return jnp.concatenate(
        [
            (
                jnp.dot(
                    allowed,
                    values[job * tokens : (job + 1) * tokens],
                    preferred_element_type=jnp.float32,
                )
                / counts
            ).astype(jnp.bfloat16)
            for job, (allowed, counts) in enumerate(masks)
        ]
    )


def home(sums):
    by_half = sums.reshape(2, 2, RING, ROWS, -1)
    down = by_half[0, 0] + moved(by_half[0, 1].astype(jnp.bfloat16), stay, 1).astype(jnp.float32)
    up16 = by_half[1].astype(jnp.bfloat16)
    up = moved(up16[0], mirror).astype(jnp.float32) + moved(up16[1], mirror, 1).astype(jnp.float32)
    return columns_back(jnp.stack([down, up], axis=1).astype(jnp.bfloat16))


def local(
    down_prev,
    up_prev,
    down_stash,
    up_stash,
    down_cot,
    up_cot,
    boundary,
    segment_ids,
    value_weight,
    output_weight,
):
    rank = lax.axis_index("pipe")
    is_first = rank == 0
    is_last = rank == RANKS - 1
    order = token_order()

    send_down = jnp.where(is_last, boundary[0], down_prev[0])
    send_up = jnp.where(is_first, boundary[1], up_prev[0])
    send_down_cot = jnp.where(is_first, boundary[2], down_cot[0])
    send_up_cot = jnp.where(is_last, boundary[3], up_cot[0])

    mirrored_ids = moved(segment_ids[:, 0], mirror)
    forward_masks = (
        segment_mask(segment_ids[0, 0], order),
        segment_mask(mirrored_ids[1], order),
    )
    backward_masks = (
        segment_mask(segment_ids[2, 0], order),
        segment_mask(mirrored_ids[3], order),
    )

    cots = columns_out(jnp.stack([send_down_cot, send_up_cot]))
    down_g, up_g = cots[:, 0], cots[:, 1]
    grad_rows = jnp.concatenate(
        [
            moved(down_g, down_one).reshape(-1, down_g.shape[-1]),
            moved(down_g, down_one, 1).reshape(-1, down_g.shape[-1]),
            moved(up_g, mirror_next).reshape(-1, up_g.shape[-1]),
            moved(up_g, mirror_next, 1).reshape(-1, up_g.shape[-1]),
        ]
    )

    head, width = output_weight.shape[2:]
    output_cols = turned(
        output_weight[0, 0].reshape(head, RING, width // RING).transpose(1, 0, 2)
    )
    value_cols = turned(value_weight[0, 0].reshape(RING, width // RING, head))

    sent = columns_out(
        jnp.stack(
            [
                normalize(send_down)[0].astype(jnp.bfloat16),
                normalize(send_up)[0].astype(jnp.bfloat16),
            ]
        )
    )
    down_x, up_x = sent[:, 0], sent[:, 1]
    forward_rows = jnp.concatenate(
        [
            moved(down_x, up_one).reshape(-1, down_x.shape[-1]),
            moved(down_x, up_one, 1).reshape(-1, down_x.shape[-1]),
            moved(up_x, mirror_prev).reshape(-1, up_x.shape[-1]),
            moved(up_x, mirror_prev, 1).reshape(-1, up_x.shape[-1]),
        ]
    )

    down_normed, down_inverse = normalize(down_stash[0])
    up_normed, up_inverse = normalize(up_stash[0])
    kept = columns_out(jnp.stack([down_normed, up_normed]).astype(jnp.bfloat16))
    down_n, up_n = kept[:, 0], kept[:, 1]
    kept_rows = jnp.concatenate(
        [
            down_n.reshape(-1, down_n.shape[-1]),
            moved(down_n, stay, 1).reshape(-1, down_n.shape[-1]),
            moved(up_n, mirror).reshape(-1, up_n.shape[-1]),
            moved(up_n, mirror, 1).reshape(-1, up_n.shape[-1]),
        ]
    )

    from_below = moved(jnp.stack([send_down, send_up_cot]), up_one)
    from_above = moved(jnp.stack([send_up, send_down_cot]), down_one)

    scaled = summed_over_ring(product("rd,hkd->hrk", grad_rows, output_cols))
    tokens = scaled.shape[0] // 2
    acts = shared(
        jnp.concatenate(
            [
                contract_rows(
                    allowed,
                    (scaled[job * tokens : (job + 1) * tokens] / counts).astype(jnp.bfloat16),
                ).astype(jnp.bfloat16)
                for job, (allowed, counts) in enumerate(backward_masks)
            ]
        )
    )
    normed_grads = home(product("hrk,hdk->rd", acts, value_cols)).astype(jnp.float32)

    def input_grad(own_grad, own_normed, own_inverse, normed_grad):
        project = jnp.mean(normed_grad * own_normed, axis=-1, keepdims=True)
        out = own_grad.astype(jnp.float32) + own_inverse * (normed_grad - own_normed * project)
        return out.astype(jnp.bfloat16)

    down_back = input_grad(from_above[1], down_normed, down_inverse, normed_grads[0])
    up_back = input_grad(from_below[1], up_normed, up_inverse, normed_grads[1])

    forward_mixed = shared(mixed_of(forward_rows, forward_masks, value_cols))
    added = home(product("hrk,hkd->rd", forward_mixed, output_cols)).astype(jnp.float32)
    down_out = (from_below[0].astype(jnp.float32) + added[0]).astype(jnp.bfloat16)
    up_out = (from_above[0].astype(jnp.float32) + added[1]).astype(jnp.bfloat16)

    value_grad = turned(product("rd,hrk->hdk", kept_rows, acts).astype(jnp.bfloat16))
    kept_mixed = shared(mixed_of(kept_rows, backward_masks, value_cols))
    output_grad = turned(product("hrk,rd->hkd", kept_mixed, grad_rows).astype(jnp.bfloat16))

    return (
        down_out[None],
        up_out[None],
        down_back[None],
        up_back[None],
        value_grad.reshape(width, head).astype(jnp.float32)[None],
        output_grad.transpose(1, 0, 2).reshape(head, width).astype(jnp.float32)[None],
    )


def contract_rows(left, right):
    return lax.dot_general(
        left, right, (((0,), (0,)), ((), ())), preferred_element_type=jnp.float32
    )


def solution(mesh):
    placed = (
        P("pipe", "tensor", None),
        P("pipe", "tensor", None),
        P("pipe", "tensor", None),
        P("pipe", "tensor", None),
        P("pipe", "tensor", None),
        P("pipe", "tensor", None),
        P(None, "tensor", None),
        P(None, "pipe", None),
        P("pipe", None, None, "tensor"),
        P("pipe", None, "tensor", None),
    )
    return jax.shard_map(
        local,
        mesh=mesh,
        in_specs=placed,
        out_specs=(
            P("pipe", "tensor", None),
            P("pipe", "tensor", None),
            P("pipe", "tensor", None),
            P("pipe", "tensor", None),
            P("pipe", None, "tensor"),
            P("pipe", "tensor", None),
        ),
        check_vma=False,
    )
```

profile of v0, /device:TPU:96, one launch (start us, length us, event | category | flops | bytes accessed | tf_op | source)
XLA Modules:
  0.0 339.5 jit_solution(12490156272451843226)
XLA Ops:
  2.2 1.2 slice_select_fusion
  5.1 4.6 %all-to-all-start.6 = ((bf16[4,2,32,1024]{3,2,1,0:T(8,128)(2,1)}), bf16[4,2,32,1024]{3,2,1,0:T(8,128)(2,1)S(1)}, u32[]{:S(2)}, u32[]{:S(2)}) async-start(bf16[4,2,32,1024]{3,2,1,0:T(8,128)(2,1)} %copy.90), calls=%async_computation.6 | async-start | bytes 1048576 | tf_op jit(solution)/shard_map/all_to_all | solution.py:53
  14.6 2.3 slice.149
  17.1 3.0 all-to-all-done.6
  20.1 3.5 %all-to-all-start = ((bf16[4,2,32,1024]{3,2,1,0:T(8,128)(2,1)}), bf16[4,2,32,1024]{3,2,1,0:T(8,128)(2,1)S(1)}, u32[]{:S(2)}, u32[]{:S(2)}) async-start(bf16[4,2,32,1024]{3,2,1,0:T(8,128)(2,1)} %copy.83), calls=%async_computation | async-start | bytes 1048576 | tf_op jit(solution)/shard_map/all_to_all | solution.py:53
  24.4 8.7 %all-to-all-done = bf16[4,2,32,1024]{3,2,1,0:T(8,128)(2,1)S(1)} async-done(((bf16[4,2,32,1024]{3,2,1,0:T(8,128)(2,1)}), bf16[4,2,32,1024]{3,2,1,0:T(8,128)(2,1)S(1)}, u32[]{:S(2)}, u32[]{:S(2)}) %all-to-all-start) | async-done | bytes 524320 | tf_op jit(solution)/shard_map/all_to_all | solution.py:53
  33.9 3.6 %all-to-all-start.1 = ((bf16[4,1024,128]{2,1,0:T(8,128)(2,1)}), bf16[4,1024,128]{2,1,0:T(8,128)(2,1)S(1)}, u32[]{:S(2)}, u32[]{:S(2)}) async-start(bf16[4,1024,128]{2,1,0:T(8,128)(2,1)} %bitcast.11), calls=%async_computation.1 | async-start | bytes 2097152 | tf_op jit(solution)/shard_map/all_to_all | solution.py:53
  39.1 1.3 copy.86
  40.6 11.2 %all-to-all-done.1 = bf16[4,1024,128]{2,1,0:T(8,128)(2,1)S(1)} async-done(((bf16[4,1024,128]{2,1,0:T(8,128)(2,1)}), bf16[4,1024,128]{2,1,0:T(8,128)(2,1)S(1)}, u32[]{:S(2)}, u32[]{:S(2)}) %all-to-all-start.1) | async-done | bytes 1048608 | tf_op jit(solution)/shard_map/all_to_all | solution.py:53
  51.8 3.5 %all-to-all-start.4 = ((bf16[4,128,1024]{2,1,0:T(8,128)(2,1)}), bf16[4,128,1024]{2,1,0:T(8,128)(2,1)S(1)}, u32[]{:S(2)}, u32[]{:S(2)}) async-start(bf16[4,128,1024]{2,1,0:T(8,128)(2,1)} %bitcast.15), calls=%async_computation.4 | async-start | bytes 2097152 | tf_op jit(solution)/shard_map/all_to_all | solution.py:53
  56.2 4.6 %collective-permute-start.2 = (bf16[4,32,1024]{2,1,0:T(8,128)(2,1)}, bf16[4,32,1024]{2,1,0:T(8,128)(2,1)}, u32[]{:S(2)}, u32[]{:S(2)}) collective-permute-start(bf16[4,32,1024]{2,1,0:T(8,128)(2,1)} %get-tuple-element.65), channel_id=1, source_target_pairs={{0,9},{1,8},{2,11},{3,10},{4,13},{5,12},{6,15},{7,14},{8,17},{9,16... | collective-permute-start | bytes 786440 | tf_op jit(solution)/shard_map/ppermute | solution.py:25
  60.8 2.4 collective-permute-start.1
  63.2 2.7 collective-permute-start.3
  66.3 10.9 %collective-permute-done.2 = bf16[4,32,1024]{2,1,0:T(8,128)(2,1)} collective-permute-done((bf16[4,32,1024]{2,1,0:T(8,128)(2,1)}, bf16[4,32,1024]{2,1,0:T(8,128)(2,1)}, u32[]{:S(2)}, u32[]{:S(2)}) %collective-permute-start.2) | collective-permute-done | bytes 262176 | tf_op jit(solution)/shard_map/ppermute | solution.py:25
  77.2 3.1 collective-permute-start.10
  80.3 7.9 %collective-permute-done.4 = bf16[4,32,1024]{2,1,0:T(8,128)(2,1)} collective-permute-done((bf16[4,32,1024]{2,1,0:T(8,128)(2,1)}, bf16[4,32,1024]{2,1,0:T(8,128)(2,1)}, u32[]{:S(2)}, u32[]{:S(2)}) %collective-permute-start.4) | collective-permute-done | bytes 262176 | tf_op jit(solution)/shard_map/ppermute | solution.py:25
  88.3 7.0 %collective-permute-start.13 = (bf16[4,32,1024]{2,1,0:T(8,128)(2,1)S(1)}, bf16[4,32,1024]{2,1,0:T(8,128)(2,1)}, u32[]{:S(2)}, u32[]{:S(2)}) collective-permute-start(bf16[4,32,1024]{2,1,0:T(8,128)(2,1)S(1)} %get-tuple-element.64), channel_id=1, source_target_pairs={{0,241},{1,240},{2,243},{3,242},{4,245},{5,244},{6,247},{7,246},{8... | collective-permute-start | bytes 786440 | tf_op jit(solution)/shard_map/ppermute | solution.py:25
  95.3 1.9 collective-permute-start.12
  97.2 2.7 fusion.1
  99.9 4.5 %all-to-all-start.2 = ((bf16[4,512,128]{2,1,0:T(8,128)(2,1)}), bf16[4,512,128]{2,1,0:T(8,128)(2,1)S(1)}, u32[]{:S(2)}, u32[]{:S(2)}) async-start(bf16[4,512,128]{2,1,0:T(8,128)(2,1)} %fusion.1), calls=%async_computation.2 | async-start | bytes 1048576 | tf_op jit(solution)/shard_map/all_to_all | solution.py:53
  105.3 1.3 collective-permute-start
  106.6 9.1 %collective-permute-done.13 = bf16[4,32,1024]{2,1,0:T(8,128)(2,1)} collective-permute-done((bf16[4,32,1024]{2,1,0:T(8,128)(2,1)S(1)}, bf16[4,32,1024]{2,1,0:T(8,128)(2,1)}, u32[]{:S(2)}, u32[]{:S(2)}) %collective-permute-start.13) | collective-permute-done | bytes 262176 | tf_op jit(solution)/shard_map/ppermute | solution.py:25
  115.7 2.7 fusion.2
  118.5 4.8 %all-to-all-start.7 = ((bf16[4,512,128]{2,1,0:T(8,128)(2,1)}), bf16[4,512,128]{2,1,0:T(8,128)(2,1)S(1)}, u32[]{:S(2)}, u32[]{:S(2)}) async-start(bf16[4,512,128]{2,1,0:T(8,128)(2,1)} %fusion.2), calls=%async_computation.7 | async-start | bytes 1048576 | tf_op jit(solution)/shard_map/all_to_all | solution.py:53
  125.3 6.5 %all-to-all-done.7 = bf16[4,512,128]{2,1,0:T(8,128)(2,1)S(1)} async-done(((bf16[4,512,128]{2,1,0:T(8,128)(2,1)}), bf16[4,512,128]{2,1,0:T(8,128)(2,1)S(1)}, u32[]{:S(2)}, u32[]{:S(2)}) %all-to-all-start.7) | async-done | bytes 524320 | tf_op jit(solution)/shard_map/all_to_all | solution.py:53
  132.6 3.5 %all-to-all-start.3 = ((bf16[4,512,128]{2,1,0:T(8,128)(2,1)}), bf16[4,512,128]{2,1,0:T(8,128)(2,1)S(1)}, u32[]{:S(2)}, u32[]{:S(2)}) async-start(bf16[4,512,128]{2,1,0:T(8,128)(2,1)} %broadcast_in_dim.6), calls=%async_computation.3 | async-start | bytes 1048576 | tf_op jit(solution)/shard_map/all_to_all | solution.py:53
  137.6 6.5 %all-to-all-done.3 = bf16[4,512,128]{2,1,0:T(8,128)(2,1)S(1)} async-done(((bf16[4,512,128]{2,1,0:T(8,128)(2,1)}), bf16[4,512,128]{2,1,0:T(8,128)(2,1)S(1)}, u32[]{:S(2)}, u32[]{:S(2)}) %all-to-all-start.3) | async-done | bytes 524320 | tf_op jit(solution)/shard_map/all_to_all | solution.py:53
  145.1 4.1 %all-to-all-start.8 = ((bf16[4,512,128]{2,1,0:T(8,128)(2,1)}), bf16[4,512,128]{2,1,0:T(8,128)(2,1)}, u32[]{:S(2)}, u32[]{:S(2)}) async-start(bf16[4,512,128]{2,1,0:T(8,128)(2,1)} %broadcast_in_dim.7), calls=%async_computation.8 | async-start | bytes 1048576 | tf_op jit(solution)/shard_map/all_to_all | solution.py:53
  149.3 1.8 bitcast_convert_fusion.1
  151.0 1.3 copy-done
  153.1 2.3 collective-permute-start.6
  156.2 2.4 collective-permute-start.8
  158.7 3.6 %collective-permute-start.7 = (bf16[4,32,1024]{2,1,0:T(8,128)(2,1)}, bf16[4,32,1024]{2,1,0:T(8,128)(2,1)}, u32[]{:S(2)}, u32[]{:S(2)}) collective-permute-start(bf16[4,32,1024]{2,1,0:T(8,128)(2,1)} %bitcast.22), channel_id=1, source_target_pairs={{0,248},{1,249},{2,250},{3,251},{4,252},{5,253},{6,254},{7,255},{8... | collective-permute-start | bytes 786440 | tf_op jit(solution)/shard_map/ppermute | solution.py:25
  162.3 1.8 bitcast_convert_fusion
  166.7 1.2 collective-permute-start.14
  167.9 1.2 fusion.46
  169.1 11.4 %collective-permute-done.8 = bf16[4,32,1024]{2,1,0:T(8,128)(2,1)} collective-permute-done((bf16[4,32,1024]{2,1,0:T(8,128)(2,1)}, bf16[4,32,1024]{2,1,0:T(8,128)(2,1)}, u32[]{:S(2)}, u32[]{:S(2)}) %collective-permute-start.8) | collective-permute-done | bytes 262176 | tf_op jit(solution)/shard_map/ppermute | solution.py:25
  180.5 5.5 %collective-permute-start.16 = (bf16[4,32,1024]{2,1,0:T(8,128)(2,1)}, bf16[4,32,1024]{2,1,0:T(8,128)(2,1)}, u32[]{:S(2)}, u32[]{:S(2)}) collective-permute-start(bf16[4,32,1024]{2,1,0:T(8,128)(2,1)} %bitcast.45), channel_id=1, source_target_pairs={{0,249},{1,248},{2,251},{3,250},{4,253},{5,252},{6,255},{7,254},{8... | collective-permute-start | bytes 786440 | tf_op jit(solution)/shard_map/ppermute | solution.py:25
  188.0 6.0 %all-to-all-start.5 = ((bf16[4,2,32,1024]{3,2,1,0:T(8,128)(2,1)}), bf16[4,2,32,1024]{3,2,1,0:T(8,128)(2,1)}, u32[]{:S(2)}, u32[]{:S(2)}) async-start(bf16[4,2,32,1024]{3,2,1,0:T(8,128)(2,1)} %pad_maximum_fusion.1), calls=%async_computation.5 | async-start | bytes 1048576 | tf_op jit(solution)/shard_map/all_to_all | solution.py:53
  194.0 6.1 %collective-permute-done.16 = bf16[4,32,1024]{2,1,0:T(8,128)(2,1)} collective-permute-done((bf16[4,32,1024]{2,1,0:T(8,128)(2,1)}, bf16[4,32,1024]{2,1,0:T(8,128)(2,1)}, u32[]{:S(2)}, u32[]{:S(2)}) %collective-permute-start.16) | collective-permute-done | bytes 262176 | tf_op jit(solution)/shard_map/ppermute | solution.py:25
  204.2 6.8 %all-to-all-start.9 = ((bf16[4,2,32,1024]{3,2,1,0:T(8,128)(2,1)}), bf16[4,2,32,1024]{3,2,1,0:T(8,128)(2,1)S(1)}, u32[]{:S(2)}, u32[]{:S(2)}) async-start(bf16[4,2,32,1024]{3,2,1,0:T(8,128)(2,1)} %pad_maximum_fusion.3), calls=%async_computation.9 | async-start | bytes 1048576 | tf_op jit(solution)/shard_map/all_to_all | solution.py:53
  212.3 8.6 %all-to-all-done.9 = bf16[4,2,32,1024]{3,2,1,0:T(8,128)(2,1)S(1)} async-done(((bf16[4,2,32,1024]{3,2,1,0:T(8,128)(2,1)}), bf16[4,2,32,1024]{3,2,1,0:T(8,128)(2,1)S(1)}, u32[]{:S(2)}, u32[]{:S(2)}) %all-to-all-start.9) | async-done | bytes 524320 | tf_op jit(solution)/shard_map/all_to_all | solution.py:53
  223.0 2.0 fusion.25
  225.3 1.4 copy.92
  227.3 2.0 fusion.29
  230.1 11.4 %all_to_all.75 = bf16[4,2,32,1024]{3,2,1,0:T(8,128)(2,1)S(1)} all-to-all(bf16[4,2,32,1024]{3,2,1,0:T(8,128)(2,1)S(1)} %copy.96), channel_id=1, replica_groups={{0,2,4,6},{1,3,5,7},{8,10,12,14},{9,11,13,15},{16,18,20,22},{17,19,21,2..., dimensions={0} | all-to-all | bytes 1048576 | tf_op jit(solution)/shard_map/all_to_all | solution.py:53
  241.5 2.3 collective-permute-start.17
  243.8 2.7 collective-permute-start.19
  246.5 3.4 %collective-permute-start.18 = (bf16[4,32,1024]{2,1,0:T(8,128)(2,1)S(1)}, bf16[4,32,1024]{2,1,0:T(8,128)(2,1)S(1)}, u32[]{:S(2)}, u32[]{:S(2)}) collective-permute-start(bf16[4,32,1024]{2,1,0:T(8,128)(2,1)S(1)} %get-tuple-element.58), channel_id=1, source_target_pairs={{0,248},{1,249},{2,250},{3,251},{4,252},{5,253},{6,254},{7,255},{8... | collective-permute-start | bytes 786440 | tf_op jit(solution)/shard_map/ppermute | solution.py:25
  250.0 2.0 collective-permute-done.17
  252.0 11.0 %collective-permute-done.19 = bf16[4,32,1024]{2,1,0:T(8,128)(2,1)S(1)} collective-permute-done((bf16[4,32,1024]{2,1,0:T(8,128)(2,1)S(1)}, bf16[4,32,1024]{2,1,0:T(8,128)(2,1)S(1)}, u32[]{:S(2)}, u32[]{:S(2)}) %collective-permute-start.19) | collective-permute-done | bytes 262176 | tf_op jit(solution)/shard_map/ppermute | solution.py:25
  263.0 6.8 %collective-permute-done.18 = bf16[4,32,1024]{2,1,0:T(8,128)(2,1)S(1)} collective-permute-done((bf16[4,32,1024]{2,1,0:T(8,128)(2,1)S(1)}, bf16[4,32,1024]{2,1,0:T(8,128)(2,1)S(1)}, u32[]{:S(2)}, u32[]{:S(2)}) %collective-permute-start.18) | collective-permute-done | bytes 262176 | tf_op jit(solution)/shard_map/ppermute | solution.py:25
  270.5 13.2 %all_to_all.76 = bf16[4,512,128]{2,1,0:T(8,128)(2,1)S(1)} all-to-all(bf16[4,512,128]{2,1,0:T(8,128)(2,1)S(1)} %fusion.3), channel_id=1, replica_groups={{0,2,4,6},{1,3,5,7},{8,10,12,14},{9,11,13,15},{16,18,20,22},{17,19,21,2..., dimensions={0} | all-to-all | bytes 1048576 | tf_op jit(solution)/shard_map/all_to_all | solution.py:53
  285.4 3.5 %all-to-all-start.13 = ((bf16[4,512,128]{1,2,0:T(8,128)(2,1)}), bf16[4,512,128]{1,2,0:T(8,128)(2,1)S(1)}, u32[]{:S(2)}, u32[]{:S(2)}) async-start(bf16[4,512,128]{1,2,0:T(8,128)(2,1)} %broadcast_in_dim.8), calls=%async_computation.13 | async-start | bytes 1048576 | tf_op jit(solution)/shard_map/all_to_all | solution.py:53
  288.9 2.7 fusion
  291.6 7.2 %all-to-all-done.13 = bf16[4,512,128]{1,2,0:T(8,128)(2,1)S(1)} async-done(((bf16[4,512,128]{1,2,0:T(8,128)(2,1)}), bf16[4,512,128]{1,2,0:T(8,128)(2,1)S(1)}, u32[]{:S(2)}, u32[]{:S(2)}) %all-to-all-start.13) | async-done | bytes 524320 | tf_op jit(solution)/shard_map/all_to_all | solution.py:53
  298.8 3.5 %all-to-all-start.11 = ((bf16[4,1024,128]{1,2,0:T(8,128)(2,1)}), bf16[4,1024,128]{1,2,0:T(8,128)(2,1)S(1)}, u32[]{:S(2)}, u32[]{:S(2)}) async-start(bf16[4,1024,128]{1,2,0:T(8,128)(2,1)} %fusion), calls=%async_computation.11 | async-start | bytes 2097152 | tf_op jit(solution)/shard_map/all_to_all | solution.py:53
  302.4 2.9 convolution_convert_fusion
  305.2 11.9 %all-to-all-done.11 = bf16[4,1024,128]{1,2,0:T(8,128)(2,1)S(1)} async-done(((bf16[4,1024,128]{1,2,0:T(8,128)(2,1)}), bf16[4,1024,128]{1,2,0:T(8,128)(2,1)S(1)}, u32[]{:S(2)}, u32[]{:S(2)}) %all-to-all-start.11) | async-done | bytes 1048608 | tf_op jit(solution)/shard_map/all_to_all | solution.py:53
  317.1 3.5 %all-to-all-start.14 = ((bf16[4,128,1024]{2,1,0:T(8,128)(2,1)}), bf16[4,128,1024]{2,1,0:T(8,128)(2,1)S(1)}, u32[]{:S(2)}, u32[]{:S(2)}) async-start(bf16[4,128,1024]{2,1,0:T(8,128)(2,1)} %convolution_convert_fusion), calls=%async_computation.14 | async-start | bytes 2097152 | tf_op jit(solution)/shard_map/all_to_all | solution.py:53
  320.7 1.6 copy.98
  322.3 12.2 %all-to-all-done.14 = bf16[4,128,1024]{2,1,0:T(8,128)(2,1)S(1)} async-done(((bf16[4,128,1024]{2,1,0:T(8,128)(2,1)}), bf16[4,128,1024]{2,1,0:T(8,128)(2,1)S(1)}, u32[]{:S(2)}, u32[]{:S(2)}) %all-to-all-start.14) | async-done | bytes 1048608 | tf_op jit(solution)/shard_map/all_to_all | solution.py:53
  334.8 1.9 copy.100
  336.6 2.9 copy.101
  (157 shorter events, 37.0 us)
Async XLA Ops:
  1.3 39.1 %collective-permute-start.5 = (s32[4,256]{1,0:T(4,128)S(1)}, s32[4,256]{1,0:T(4,128)S(1)}, u32[]{:S(2)}, u32[]{:S(2)}) collective-permute-start(s32[4,256]{1,0:T(4,128)S(1)} %bitcast.189), channel_id=1, source_target_pairs={{0,248},{1,249},{2,250},{3,251},{4,252},{5,253},{6,254},{7,255},{8... | collective-permute-start | bytes 12296 | tf_op jit(solution)/shard_map/ppermute | solution.py:25
  3.4 6.3 %copy-start.9 = (bf16[4,32,4096]{2,1,0:T(8,128)(2,1)S(1)}, bf16[4,32,4096]{2,1,0:T(8,128)(2,1)}, u32[]{:S(2)}) copy-start(bf16[4,32,4096]{2,1,0:T(8,128)(2,1)} %param.16) | copy-start | bytes 3145732
  3.4 6.3 %copy-start.10 = (bf16[1,32,4096]{2,1,0:T(8,128)(2,1)S(1)}, bf16[1,32,4096]{2,1,0:T(8,128)(2,1)}, u32[]{:S(2)}) copy-start(bf16[1,32,4096]{2,1,0:T(8,128)(2,1)} %param.10) | copy-start | bytes 786436
  3.4 6.3 %copy-start.11 = (bf16[1,32,4096]{2,1,0:T(8,128)(2,1)S(1)}, bf16[1,32,4096]{2,1,0:T(8,128)(2,1)}, u32[]{:S(2)}) copy-start(bf16[1,32,4096]{2,1,0:T(8,128)(2,1)} %param.11) | copy-start | bytes 786436
  5.1 6.7 %copy-start.2 = (bf16[1,32,4096]{2,1,0:T(8,128)(2,1)S(1)}, bf16[1,32,4096]{2,1,0:T(8,128)(2,1)}, u32[]{:S(2)}) copy-start(bf16[1,32,4096]{2,1,0:T(8,128)(2,1)} %param.12) | copy-start | bytes 786436
  5.1 14.9 %all-to-all-start.6 = ((bf16[4,2,32,1024]{3,2,1,0:T(8,128)(2,1)}), bf16[4,2,32,1024]{3,2,1,0:T(8,128)(2,1)S(1)}, u32[]{:S(2)}, u32[]{:S(2)}) async-start(bf16[4,2,32,1024]{3,2,1,0:T(8,128)(2,1)} %copy.90), calls=%async_computation.6 | async-start | bytes 1048576 | tf_op jit(solution)/shard_map/all_to_all | solution.py:53
  10.9 216.4 %collective-permute-start.9 = (bf16[2,32,4096]{2,1,0:T(8,128)(2,1)}, bf16[2,32,4096]{2,1,0:T(8,128)(2,1)}, u32[]{:S(2)}, u32[]{:S(2)}) collective-permute-start(bf16[2,32,4096]{2,1,0:T(8,128)(2,1)} %pad_maximum_fusion.2), channel_id=1, source_target_pairs={{0,248},{1,249},{2,250},{3,251},{4,252},{5,253},{6,254},{7,255},{8... | collective-permute-start | bytes 1572872 | tf_op jit(solution)/shard_map/ppermute | solution.py:25
  13.2 3.7 %copy-start.1 = (bf16[1,32,4096]{2,1,0:T(8,128)(2,1)S(1)}, bf16[1,32,4096]{2,1,0:T(8,128)(2,1)}, u32[]{:S(2)}) copy-start(bf16[1,32,4096]{2,1,0:T(8,128)(2,1)} %param.13) | copy-start | bytes 786436
  17.1 21.0 %copy-start.13 = (s32[4,1,256]{2,1,0:T(1,128)S(1)}, s32[4,1,256]{2,1,0:T(1,128)}, u32[]{:S(2)}) copy-start(s32[4,1,256]{2,1,0:T(1,128)} %param.17) | copy-start | bytes 12292
  20.1 13.0 %copy-start.5 = (bf16[4,2,32,1024]{3,2,1,0:T(8,128)(2,1)}, bf16[4,2,32,1024]{3,2,1,0:T(8,128)(2,1)S(1)}, u32[]{:S(2)}) copy-start(bf16[4,2,32,1024]{3,2,1,0:T(8,128)(2,1)S(1)} %all-to-all-done.6) | copy-start | bytes 1572868
  20.1 13.0 %all-to-all-start = ((bf16[4,2,32,1024]{3,2,1,0:T(8,128)(2,1)}), bf16[4,2,32,1024]{3,2,1,0:T(8,128)(2,1)S(1)}, u32[]{:S(2)}, u32[]{:S(2)}) async-start(bf16[4,2,32,1024]{3,2,1,0:T(8,128)(2,1)} %copy.83), calls=%async_computation | async-start | bytes 1048576 | tf_op jit(solution)/shard_map/all_to_all | solution.py:53
  33.1 0.8 copy-start.7
  33.9 4.5 %slice-start = ((bf16[1,2,128,4096]{3,2,1,0:T(8,128)(2,1)}), bf16[1,1,128,4096]{3,2,1,0:T(8,128)(2,1)S(1)}, s32[]{:S(2)}) async-start(bf16[1,2,128,4096]{3,2,1,0:T(8,128)(2,1)} %param.19), calls=%async_computation.15 | async-start | bytes 2097152 | tf_op jit(solution)/shard_map/slice | solution.py:185
  33.9 17.9 %all-to-all-start.1 = ((bf16[4,1024,128]{2,1,0:T(8,128)(2,1)}), bf16[4,1024,128]{2,1,0:T(8,128)(2,1)S(1)}, u32[]{:S(2)}, u32[]{:S(2)}) async-start(bf16[4,1024,128]{2,1,0:T(8,128)(2,1)} %bitcast.11), calls=%async_computation.1 | async-start | bytes 2097152 | tf_op jit(solution)/shard_map/all_to_all | solution.py:53
  39.1 16.2 %copy-start.8 = (bf16[4,2,32,1024]{3,2,1,0:T(8,128)(2,1)S(1)}, bf16[4,2,32,1024]{3,2,1,0:T(8,128)(2,1)}, u32[]{:S(2)}) copy-start(bf16[4,2,32,1024]{3,2,1,0:T(8,128)(2,1)} %copy-done.7) | copy-start | bytes 1572868
  40.4 25.8 %copy-start.6 = (bf16[4,2,32,1024]{3,2,1,0:T(8,128)(2,1)S(1)}, bf16[4,2,32,1024]{3,2,1,0:T(8,128)(2,1)}, u32[]{:S(2)}) copy-start(bf16[4,2,32,1024]{3,2,1,0:T(8,128)(2,1)} %copy-done.5) | copy-start | bytes 1572868
  51.8 48.1 %all-to-all-start.4 = ((bf16[4,128,1024]{2,1,0:T(8,128)(2,1)}), bf16[4,128,1024]{2,1,0:T(8,128)(2,1)S(1)}, u32[]{:S(2)}, u32[]{:S(2)}) async-start(bf16[4,128,1024]{2,1,0:T(8,128)(2,1)} %bitcast.15), calls=%async_computation.4 | async-start | bytes 2097152 | tf_op jit(solution)/shard_map/all_to_all | solution.py:53
  56.2 21.0 %collective-permute-start.2 = (bf16[4,32,1024]{2,1,0:T(8,128)(2,1)}, bf16[4,32,1024]{2,1,0:T(8,128)(2,1)}, u32[]{:S(2)}, u32[]{:S(2)}) collective-permute-start(bf16[4,32,1024]{2,1,0:T(8,128)(2,1)} %get-tuple-element.65), channel_id=1, source_target_pairs={{0,9},{1,8},{2,11},{3,10},{4,13},{5,12},{6,15},{7,14},{8,17},{9,16... | collective-permute-start | bytes 786440 | tf_op jit(solution)/shard_map/ppermute | solution.py:25
  60.8 16.4 %collective-permute-start.1 = (bf16[4,32,1024]{2,1,0:T(8,128)(2,1)}, bf16[4,32,1024]{2,1,0:T(8,128)(2,1)}, u32[]{:S(2)}, u32[]{:S(2)}) collective-permute-start(bf16[4,32,1024]{2,1,0:T(8,128)(2,1)} %get-tuple-element.65), channel_id=1, source_target_pairs={{0,8},{1,9},{2,10},{3,11},{4,12},{5,13},{6,14},{7,15},{8,16},{9,17... | collective-permute-start | bytes 786440 | tf_op jit(solution)/shard_map/ppermute | solution.py:25
  63.2 25.1 %collective-permute-start.4 = (bf16[4,32,1024]{2,1,0:T(8,128)(2,1)}, bf16[4,32,1024]{2,1,0:T(8,128)(2,1)}, u32[]{:S(2)}, u32[]{:S(2)}) collective-permute-start(bf16[4,32,1024]{2,1,0:T(8,128)(2,1)} %get-tuple-element.66), channel_id=1, source_target_pairs={{0,1},{1,0},{2,3},{3,2},{4,5},{5,4},{6,7},{7,6},{8,249},{9,248},{1... | collective-permute-start | bytes 786440 | tf_op jit(solution)/shard_map/ppermute | solution.py:25
  63.2 32.1 %collective-permute-start.3 = (bf16[4,32,1024]{2,1,0:T(8,128)(2,1)}, bf16[4,32,1024]{2,1,0:T(8,128)(2,1)}, u32[]{:S(2)}, u32[]{:S(2)}) collective-permute-start(bf16[4,32,1024]{2,1,0:T(8,128)(2,1)} %get-tuple-element.66), channel_id=1, source_target_pairs={{0,0},{1,1},{2,2},{3,3},{4,4},{5,5},{6,6},{7,7},{8,248},{9,249},{1... | collective-permute-start | bytes 786440 | tf_op jit(solution)/shard_map/ppermute | solution.py:25
  66.2 38.1 %copy-start.12 = (s32[256]{0:T(256)}, s32[256]{0:T(256)S(1)}, u32[]{:S(2)}) copy-start(s32[256]{0:T(256)S(1)} %eq.80) | copy-start | bytes 3076
  77.2 28.1 %collective-permute-start.11 = (bf16[4,32,1024]{2,1,0:T(8,128)(2,1)S(1)}, bf16[4,32,1024]{2,1,0:T(8,128)(2,1)}, u32[]{:S(2)}, u32[]{:S(2)}) collective-permute-start(bf16[4,32,1024]{2,1,0:T(8,128)(2,1)S(1)} %get-tuple-element.63), channel_id=1, source_target_pairs={{0,249},{1,248},{2,251},{3,250},{4,253},{5,252},{6,255},{7,254},{8... | collective-permute-start | bytes 786440 | tf_op jit(solution)/shard_map/ppermute | solution.py:25
  77.2 29.4 %collective-permute-start.10 = (bf16[4,32,1024]{2,1,0:T(8,128)(2,1)S(1)}, bf16[4,32,1024]{2,1,0:T(8,128)(2,1)}, u32[]{:S(2)}, u32[]{:S(2)}) collective-permute-start(bf16[4,32,1024]{2,1,0:T(8,128)(2,1)S(1)} %get-tuple-element.63), channel_id=1, source_target_pairs={{0,248},{1,249},{2,250},{3,251},{4,252},{5,253},{6,254},{7,255},{8... | collective-permute-start | bytes 786440 | tf_op jit(solution)/shard_map/ppermute | solution.py:25
  88.3 27.5 %collective-permute-start.13 = (bf16[4,32,1024]{2,1,0:T(8,128)(2,1)S(1)}, bf16[4,32,1024]{2,1,0:T(8,128)(2,1)}, u32[]{:S(2)}, u32[]{:S(2)}) collective-permute-start(bf16[4,32,1024]{2,1,0:T(8,128)(2,1)S(1)} %get-tuple-element.64), channel_id=1, source_target_pairs={{0,241},{1,240},{2,243},{3,242},{4,245},{5,244},{6,247},{7,246},{8... | collective-permute-start | bytes 786440 | tf_op jit(solution)/shard_map/ppermute | solution.py:25
  95.3 20.5 %collective-permute-start.12 = (bf16[4,32,1024]{2,1,0:T(8,128)(2,1)S(1)}, bf16[4,32,1024]{2,1,0:T(8,128)(2,1)}, u32[]{:S(2)}, u32[]{:S(2)}) collective-permute-start(bf16[4,32,1024]{2,1,0:T(8,128)(2,1)S(1)} %get-tuple-element.64), channel_id=1, source_target_pairs={{0,240},{1,241},{2,242},{3,243},{4,244},{5,245},{6,246},{7,247},{8... | collective-permute-start | bytes 786440 | tf_op jit(solution)/shard_map/ppermute | solution.py:25
  99.9 18.6 %all-to-all-start.2 = ((bf16[4,512,128]{2,1,0:T(8,128)(2,1)}), bf16[4,512,128]{2,1,0:T(8,128)(2,1)S(1)}, u32[]{:S(2)}, u32[]{:S(2)}) async-start(bf16[4,512,128]{2,1,0:T(8,128)(2,1)} %fusion.1), calls=%async_computation.2 | async-start | bytes 1048576 | tf_op jit(solution)/shard_map/all_to_all | solution.py:53
  105.3 117.6 %collective-permute-start = (bf16[2,32,4096]{2,1,0:T(8,128)(2,1)}, bf16[2,32,4096]{2,1,0:T(8,128)(2,1)}, u32[]{:S(2)}, u32[]{:S(2)}) collective-permute-start(bf16[2,32,4096]{2,1,0:T(8,128)(2,1)} %pad_maximum_fusion), channel_id=1, source_target_pairs={{0,8},{1,9},{2,10},{3,11},{4,12},{5,13},{6,14},{7,15},{8,16},{9,17... | collective-permute-start | bytes 1572872 | tf_op jit(solution)/shard_map/ppermute | solution.py:25
  118.5 13.3 %all-to-all-start.7 = ((bf16[4,512,128]{2,1,0:T(8,128)(2,1)}), bf16[4,512,128]{2,1,0:T(8,128)(2,1)S(1)}, u32[]{:S(2)}, u32[]{:S(2)}) async-start(bf16[4,512,128]{2,1,0:T(8,128)(2,1)} %fusion.2), calls=%async_computation.7 | async-start | bytes 1048576 | tf_op jit(solution)/shard_map/all_to_all | solution.py:53
  124.3 12.9 %copy-start.16 = (f32[256]{0:T(256)S(1)}, f32[256]{0:T(256)}, u32[]{:S(2)}) copy-start(f32[256]{0:T(256)} %get-tuple-element.34) | copy-start | bytes 3076
  132.6 11.5 %all-to-all-start.3 = ((bf16[4,512,128]{2,1,0:T(8,128)(2,1)}), bf16[4,512,128]{2,1,0:T(8,128)(2,1)S(1)}, u32[]{:S(2)}, u32[]{:S(2)}) async-start(bf16[4,512,128]{2,1,0:T(8,128)(2,1)} %broadcast_in_dim.6), calls=%async_computation.3 | async-start | bytes 1048576 | tf_op jit(solution)/shard_map/all_to_all | solution.py:53
  144.1 1.0 copy-start.4
  145.1 17.2 %all-to-all-start.8 = ((bf16[4,512,128]{2,1,0:T(8,128)(2,1)}), bf16[4,512,128]{2,1,0:T(8,128)(2,1)}, u32[]{:S(2)}, u32[]{:S(2)}) async-start(bf16[4,512,128]{2,1,0:T(8,128)(2,1)} %broadcast_in_dim.7), calls=%async_computation.8 | async-start | bytes 1048576 | tf_op jit(solution)/shard_map/all_to_all | solution.py:53
  151.0 1.3 copy-start
  153.1 13.6 %collective-permute-start.6 = (bf16[4,32,1024]{2,1,0:T(8,128)(2,1)}, bf16[4,32,1024]{2,1,0:T(8,128)(2,1)}, u32[]{:S(2)}, u32[]{:S(2)}) collective-permute-start(bf16[4,32,1024]{2,1,0:T(8,128)(2,1)} %fusion.47), channel_id=1, source_target_pairs={{0,1},{1,0},{2,3},{3,2},{4,5},{5,4},{6,7},{7,6},{8,9},{9,8},{10,11... | collective-permute-start | bytes 786440 | tf_op jit(solution)/shard_map/ppermute | solution.py:25
  156.2 24.3 %collective-permute-start.8 = (bf16[4,32,1024]{2,1,0:T(8,128)(2,1)}, bf16[4,32,1024]{2,1,0:T(8,128)(2,1)}, u32[]{:S(2)}, u32[]{:S(2)}) collective-permute-start(bf16[4,32,1024]{2,1,0:T(8,128)(2,1)} %bitcast.23), channel_id=1, source_target_pairs={{0,249},{1,248},{2,251},{3,250},{4,253},{5,252},{6,255},{7,254},{8... | collective-permute-start | bytes 786440 | tf_op jit(solution)/shard_map/ppermute | solution.py:25
  158.7 27.3 %collective-permute-start.7 = (bf16[4,32,1024]{2,1,0:T(8,128)(2,1)}, bf16[4,32,1024]{2,1,0:T(8,128)(2,1)}, u32[]{:S(2)}, u32[]{:S(2)}) collective-permute-start(bf16[4,32,1024]{2,1,0:T(8,128)(2,1)} %bitcast.22), channel_id=1, source_target_pairs={{0,248},{1,249},{2,250},{3,251},{4,252},{5,253},{6,254},{7,255},{8... | collective-permute-start | bytes 786440 | tf_op jit(solution)/shard_map/ppermute | solution.py:25
  166.7 35.6 %collective-permute-start.14 = (bf16[4,32,1024]{2,1,0:T(8,128)(2,1)}, bf16[4,32,1024]{2,1,0:T(8,128)(2,1)}, u32[]{:S(2)}, u32[]{:S(2)}) collective-permute-start(bf16[4,32,1024]{2,1,0:T(8,128)(2,1)} %fusion.49), channel_id=1, source_target_pairs={{0,1},{1,0},{2,3},{3,2},{4,5},{5,4},{6,7},{7,6},{8,9},{9,8},{10,11... | collective-permute-start | bytes 786440 | tf_op jit(solution)/shard_map/ppermute | solution.py:25
  180.5 19.6 %collective-permute-start.16 = (bf16[4,32,1024]{2,1,0:T(8,128)(2,1)}, bf16[4,32,1024]{2,1,0:T(8,128)(2,1)}, u32[]{:S(2)}, u32[]{:S(2)}) collective-permute-start(bf16[4,32,1024]{2,1,0:T(8,128)(2,1)} %bitcast.45), channel_id=1, source_target_pairs={{0,249},{1,248},{2,251},{3,250},{4,253},{5,252},{6,255},{7,254},{8... | collective-permute-start | bytes 786440 | tf_op jit(solution)/shard_map/ppermute | solution.py:25
  186.0 15.2 %collective-permute-start.15 = (bf16[4,32,1024]{2,1,0:T(8,128)(2,1)}, bf16[4,32,1024]{2,1,0:T(8,128)(2,1)}, u32[]{:S(2)}, u32[]{:S(2)}) collective-permute-start(bf16[4,32,1024]{2,1,0:T(8,128)(2,1)} %bitcast.44), channel_id=1, source_target_pairs={{0,248},{1,249},{2,250},{3,251},{4,252},{5,253},{6,254},{7,255},{8... | collective-permute-start | bytes 786440 | tf_op jit(solution)/shard_map/ppermute | solution.py:25
  188.0 16.2 %all-to-all-start.5 = ((bf16[4,2,32,1024]{3,2,1,0:T(8,128)(2,1)}), bf16[4,2,32,1024]{3,2,1,0:T(8,128)(2,1)}, u32[]{:S(2)}, u32[]{:S(2)}) async-start(bf16[4,2,32,1024]{3,2,1,0:T(8,128)(2,1)} %pad_maximum_fusion.1), calls=%async_computation.5 | async-start | bytes 1048576 | tf_op jit(solution)/shard_map/all_to_all | solution.py:53
  204.2 16.6 %all-to-all-start.9 = ((bf16[4,2,32,1024]{3,2,1,0:T(8,128)(2,1)}), bf16[4,2,32,1024]{3,2,1,0:T(8,128)(2,1)S(1)}, u32[]{:S(2)}, u32[]{:S(2)}) async-start(bf16[4,2,32,1024]{3,2,1,0:T(8,128)(2,1)} %pad_maximum_fusion.3), calls=%async_computation.9 | async-start | bytes 1048576 | tf_op jit(solution)/shard_map/all_to_all | solution.py:53
  222.0 0.7 copy-start.15
  225.1 2.0 copy-start.3
  225.1 2.0 copy-start.14
  241.5 10.4 %collective-permute-start.17 = (bf16[4,32,1024]{2,1,0:T(8,128)(2,1)S(1)}, bf16[4,32,1024]{2,1,0:T(8,128)(2,1)S(1)}, u32[]{:S(2)}, u32[]{:S(2)}) collective-permute-start(bf16[4,32,1024]{2,1,0:T(8,128)(2,1)S(1)} %get-tuple-element.57), channel_id=1, source_target_pairs={{0,1},{1,0},{2,3},{3,2},{4,5},{5,4},{6,7},{7,6},{8,9},{9,8},{10,11... | collective-permute-start | bytes 786440 | tf_op jit(solution)/shard_map/ppermute | solution.py:25
  243.8 19.2 %collective-permute-start.19 = (bf16[4,32,1024]{2,1,0:T(8,128)(2,1)S(1)}, bf16[4,32,1024]{2,1,0:T(8,128)(2,1)S(1)}, u32[]{:S(2)}, u32[]{:S(2)}) collective-permute-start(bf16[4,32,1024]{2,1,0:T(8,128)(2,1)S(1)} %get-tuple-element.58), channel_id=1, source_target_pairs={{0,249},{1,248},{2,251},{3,250},{4,253},{5,252},{6,255},{7,254},{8... | collective-permute-start | bytes 786440 | tf_op jit(solution)/shard_map/ppermute | solution.py:25
  246.5 23.2 %collective-permute-start.18 = (bf16[4,32,1024]{2,1,0:T(8,128)(2,1)S(1)}, bf16[4,32,1024]{2,1,0:T(8,128)(2,1)S(1)}, u32[]{:S(2)}, u32[]{:S(2)}) collective-permute-start(bf16[4,32,1024]{2,1,0:T(8,128)(2,1)S(1)} %get-tuple-element.58), channel_id=1, source_target_pairs={{0,248},{1,249},{2,250},{3,251},{4,252},{5,253},{6,254},{7,255},{8... | collective-permute-start | bytes 786440 | tf_op jit(solution)/shard_map/ppermute | solution.py:25
  263.0 7.5 %copy-start.18 = (bf16[4,32,1024]{2,1,0:T(8,128)(2,1)}, bf16[4,32,1024]{2,1,0:T(8,128)(2,1)S(1)}, u32[]{:S(2)}) copy-start(bf16[4,32,1024]{2,1,0:T(8,128)(2,1)S(1)} %collective-permute-done.19) | copy-start | bytes 786436
  269.8 0.7 copy-start.20
  269.8 14.1 %copy-start.17 = (f32[256]{0:T(256)S(1)}, f32[256]{0:T(256)}, u32[]{:S(2)}) copy-start(f32[256]{0:T(256)} %get-tuple-element.37) | copy-start | bytes 3076
  283.8 5.1 %copy-start.19 = (bf16[4,32,1024]{2,1,0:T(8,128)(2,1)S(1)}, bf16[4,32,1024]{2,1,0:T(8,128)(2,1)}, u32[]{:S(2)}) copy-start(bf16[4,32,1024]{2,1,0:T(8,128)(2,1)} %copy-done.18) | copy-start | bytes 786436
  283.8 5.1 %copy-start.21 = (bf16[4,32,1024]{2,1,0:T(8,128)(2,1)S(1)}, bf16[4,32,1024]{2,1,0:T(8,128)(2,1)}, u32[]{:S(2)}) copy-start(bf16[4,32,1024]{2,1,0:T(8,128)(2,1)} %copy-done.20) | copy-start | bytes 786436
  285.4 13.5 %all-to-all-start.13 = ((bf16[4,512,128]{1,2,0:T(8,128)(2,1)}), bf16[4,512,128]{1,2,0:T(8,128)(2,1)S(1)}, u32[]{:S(2)}, u32[]{:S(2)}) async-start(bf16[4,512,128]{1,2,0:T(8,128)(2,1)} %broadcast_in_dim.8), calls=%async_computation.13 | async-start | bytes 1048576 | tf_op jit(solution)/shard_map/all_to_all | solution.py:53
  298.8 18.3 %all-to-all-start.11 = ((bf16[4,1024,128]{1,2,0:T(8,128)(2,1)}), bf16[4,1024,128]{1,2,0:T(8,128)(2,1)S(1)}, u32[]{:S(2)}, u32[]{:S(2)}) async-start(bf16[4,1024,128]{1,2,0:T(8,128)(2,1)} %fusion), calls=%async_computation.11 | async-start | bytes 2097152 | tf_op jit(solution)/shard_map/all_to_all | solution.py:53
  317.1 17.4 %all-to-all-start.14 = ((bf16[4,128,1024]{2,1,0:T(8,128)(2,1)}), bf16[4,128,1024]{2,1,0:T(8,128)(2,1)S(1)}, u32[]{:S(2)}, u32[]{:S(2)}) async-start(bf16[4,128,1024]{2,1,0:T(8,128)(2,1)} %convolution_convert_fusion), calls=%async_computation.14 | async-start | bytes 2097152 | tf_op jit(solution)/shard_map/all_to_all | solution.py:53
where the time goes:
time: 341 us; the launch traced here: 340 us
  waiting for transfers between devices  143 us (42%)
  starting transfers between devices  104 us (30%)
  local copies, waits for them, and re-layouts  28 us (8%)
  blocking collectives  24.6 us (7%)
  other arithmetic  19.6 us (6%)
  matrix products  19.1 us (6%)
    all_to_all x13, waiting for transfers between devices, turned(): lax.all_to_all(blocks, 'tensor', split_axis=0, concat_axis=0, axis_index_...  75.8 us
    ppermute x20, waiting for transfers between devices, moved(): return lax.ppermute(shard, ('pipe', 'tensor'), pairs)  67.6 us
    all_to_all x13, starting transfers between devices, turned(): lax.all_to_all(blocks, 'tensor', split_axis=0, concat_axis=0, axis_index_...  55.4 us
    ppermute x20, starting transfers between devices, moved(): return lax.ppermute(shard, ('pipe', 'tensor'), pairs)  48.2 us
    all_to_all x2, blocking collectives, turned(): lax.all_to_all(blocks, 'tensor', split_axis=0, concat_axis=0, axis_index_...  24.6 us
    dot_general x7, matrix products, product(): return jnp.einsum(spec, left, right, preferred_element_type=jnp.float32)  15.3 us
    unnamed x50, local copies, waits for them, and re-layouts  7.14 us
  transfers between devices with their start and end apart: 33, of which 19 were waited for; matrix products, arithmetic and copies ran while one was open for 16% of the time, Pallas kernels for 0%

commit v1 on v0

v1 whole, which is shorter than its diff:
```python
import jax
import jax.numpy as jnp
from jax import lax
from jax.sharding import PartitionSpec as P

eps = 1e-05

RANKS = 32
LANES = 8
RING = 4
ROWS = 32


def spot(rank, row, half):
    return (rank % RANKS) * LANES + (row % RING) * 2 + half % 2


def moved(shard, rank_to, half_by=0):
    pairs = [
        (spot(r, y, z), spot(rank_to(r), y, z + half_by))
        for r in range(RANKS)
        for y in range(RING)
        for z in range(2)
    ]
    return lax.ppermute(shard, ("pipe", "tensor"), pairs)


def stay(r):
    return r


def up_one(r):
    return r + 1


def down_one(r):
    return r - 1


def mirror(r):
    return RANKS - 1 - r


def mirror_next(r):
    return RANKS - 2 - r


def turned(blocks):
    return lax.all_to_all(
        blocks,
        "tensor",
        split_axis=0,
        concat_axis=0,
        axis_index_groups=[[0, 2, 4, 6], [1, 3, 5, 7]],
        tiled=True,
    )


def after(array, earlier):
    return lax.optimization_barrier((array, earlier))[0]


def to_ring(block):
    return jnp.broadcast_to(block[None], (RING,) + block.shape)


def by_columns(arrays):
    rows = jnp.concatenate(arrays)
    n, d = rows.shape
    return rows.reshape(n, RING, d // RING).transpose(1, 0, 2)


def rows_of(*pieces):
    return jnp.concatenate([piece.reshape(-1, piece.shape[-1]) for piece in pieces])


def normalize(inputs):
    widened = inputs.astype(jnp.float32)
    inverse_rms = lax.rsqrt(jnp.mean(widened * widened, axis=-1, keepdims=True) + eps)
    return (widened * inverse_rms, inverse_rms)


def product(spec, left, right):
    return jnp.einsum(spec, left, right, preferred_element_type=jnp.float32)


def token_order():
    half = lax.axis_index("tensor") % 2
    halves = jnp.stack([half, 1 - half])
    rows = jnp.arange(RING, dtype=jnp.int32)
    within = jnp.arange(ROWS, dtype=jnp.int32)
    lanes = rows[None, :] * 2 + halves[:, None]
    return (lanes[:, :, None] * ROWS + within[None, None, :]).reshape(-1)


def segment_mask(segment_row, order):
    by_half = segment_row.reshape(RING, 2, ROWS).transpose(1, 0, 2)
    half = lax.axis_index("tensor") % 2
    segments = jnp.where(half == 0, by_half, by_half[::-1]).reshape(-1)
    causal = order[:, None] >= order[None, :]
    same_segment = segments[:, None] == segments[None, :]
    allowed = jnp.logical_and(causal, same_segment)
    return (
        allowed.astype(jnp.bfloat16),
        jnp.sum(allowed.astype(jnp.float32), axis=1, keepdims=True),
    )


def ring_sum(parts):
    return jnp.sum(parts.astype(jnp.float32), axis=0)


def mixed_of(sums, masks):
    values = sums.astype(jnp.bfloat16)
    tokens = values.shape[0] // 2
    return jnp.concatenate(
        [
            (
                jnp.dot(
                    allowed,
                    values[job * tokens : (job + 1) * tokens],
                    preferred_element_type=jnp.float32,
                )
                / counts
            ).astype(jnp.bfloat16)
            for job, (allowed, counts) in enumerate(masks)
        ]
    )


def home(sums):
    by_half = sums.reshape(2, 2, RING, ROWS, -1)
    down = by_half[0, 0] + moved(by_half[0, 1].astype(jnp.bfloat16), stay, 1).astype(jnp.float32)
    up16 = by_half[1].astype(jnp.bfloat16)
    up = moved(up16[0], mirror).astype(jnp.float32) + moved(up16[1], mirror, 1).astype(jnp.float32)
    return jnp.concatenate([down, up], axis=1)


def local(
    down_prev,
    up_prev,
    down_stash,
    up_stash,
    down_cot,
    up_cot,
    boundary,
    segment_ids,
    value_weight,
    output_weight,
):
    rank = lax.axis_index("pipe")
    is_first = rank == 0
    is_last = rank == RANKS - 1
    order = token_order()

    send_down = jnp.where(is_last, boundary[0], down_prev[0])
    send_up = jnp.where(is_first, boundary[1], up_prev[0])
    send_down_cot = jnp.where(is_first, boundary[2], down_cot[0])
    send_up_cot = jnp.where(is_last, boundary[3], up_cot[0])
    head, width = output_weight.shape[2:]
    part = width // RING

    mirrored_ids = moved(segment_ids[:, 0], mirror)

    from_below = moved(jnp.concatenate([send_down, send_up_cot]), up_one)
    from_above = moved(jnp.concatenate([send_up, send_down_cot]), down_one)
    down_in, up_g_own = from_below[:ROWS], from_below[ROWS:]
    up_in, down_g_own = from_above[:ROWS], from_above[ROWS:]

    cots = turned(by_columns([send_down_cot, send_up_cot]))
    down_g, up_g = cots[:, :ROWS], cots[:, ROWS:]
    grad_rows = rows_of(
        moved(down_g, down_one),
        moved(down_g, down_one, 1),
        moved(up_g, mirror_next),
        moved(up_g, mirror_next, 1),
    )

    down_normed, down_inverse = normalize(down_stash[0])
    up_normed, up_inverse = normalize(up_stash[0])
    normed = [normalize(down_in)[0], normalize(up_in)[0], down_normed, up_normed]
    sent = turned(
        after(
            by_columns([n.astype(jnp.bfloat16) for n in normed] + [output_weight[0, 0]]), cots
        )
    )
    down_x, up_x, down_n, up_n = (sent[:, i * ROWS : (i + 1) * ROWS] for i in range(4))
    output_cols = sent[:, 4 * ROWS :]
    forward_rows = rows_of(down_x, moved(down_x, stay, 1), moved(up_x, mirror), moved(up_x, mirror, 1))
    kept_rows = rows_of(down_n, moved(down_n, stay, 1), moved(up_n, mirror), moved(up_n, mirror, 1))

    forward_masks = (
        segment_mask(segment_ids[0, 0], order),
        segment_mask(mirrored_ids[1], order),
    )
    backward_masks = (
        segment_mask(segment_ids[2, 0], order),
        segment_mask(mirrored_ids[3], order),
    )

    scaled_parts = product("rd,hkd->hrk", grad_rows, output_cols).astype(jnp.bfloat16)
    got = turned(
        after(
            jnp.concatenate([value_weight[0, 0].reshape(RING, part, head), scaled_parts], axis=1),
            sent,
        )
    )
    value_cols, scaled = got[:, :part], ring_sum(got[:, part:])
    tokens = scaled.shape[0] // 2
    act = jnp.concatenate(
        [
            contract_rows(
                allowed,
                (scaled[job * tokens : (job + 1) * tokens] / counts).astype(jnp.bfloat16),
            ).astype(jnp.bfloat16)
            for job, (allowed, counts) in enumerate(backward_masks)
        ]
    )

    forward_parts = product("rd,hdk->hrk", forward_rows, value_cols).astype(jnp.bfloat16)
    got = turned(jnp.concatenate([to_ring(act), forward_parts], axis=1))
    acts, forward_values = got[:, : 2 * tokens], ring_sum(got[:, 2 * tokens :])
    normed_grads = home(product("hrk,hdk->rd", acts, value_cols))

    forward_mixed = mixed_of(forward_values, forward_masks)
    kept_parts = product("rd,hdk->hrk", kept_rows, value_cols).astype(jnp.bfloat16)
    got = turned(jnp.concatenate([to_ring(forward_mixed), kept_parts], axis=1))
    forward_mixes, kept_values = got[:, : 2 * tokens], ring_sum(got[:, 2 * tokens :])
    added = home(product("hrk,hkd->rd", forward_mixes, output_cols))

    kept_mixed = mixed_of(kept_values, backward_masks)
    value_grad = product("rd,hrk->hdk", kept_rows, acts).astype(jnp.bfloat16)
    got = turned(jnp.concatenate([to_ring(kept_mixed), value_grad], axis=1))
    kept_mixes, value_grad = got[:, : 2 * tokens], got[:, 2 * tokens :]

    output_grad = product("hrk,rd->hkd", kept_mixes, grad_rows)
    got = turned(jnp.concatenate([normed_grads, added, output_grad], axis=1).astype(jnp.bfloat16))
    output_grad = got[:, 4 * ROWS :]
    back = got[:, : 4 * ROWS].astype(jnp.float32)
    back = back.reshape(RING, 4, ROWS, part).transpose(1, 2, 0, 3).reshape(4, ROWS, width)

    def input_grad(own_grad, own_normed, own_inverse, normed_grad):
        project = jnp.mean(normed_grad * own_normed, axis=-1, keepdims=True)
        out = own_grad.astype(jnp.float32) + own_inverse * (normed_grad - own_normed * project)
        return out.astype(jnp.bfloat16)

    down_back = input_grad(down_g_own, down_normed, down_inverse, back[0])
    up_back = input_grad(up_g_own, up_normed, up_inverse, back[1])
    down_out = (down_in.astype(jnp.float32) + back[2]).astype(jnp.bfloat16)
    up_out = (up_in.astype(jnp.float32) + back[3]).astype(jnp.bfloat16)

    return (
        down_out[None],
        up_out[None],
        down_back[None],
        up_back[None],
        value_grad.reshape(width, head).astype(jnp.float32)[None],
        output_grad.transpose(1, 0, 2).reshape(head, width).astype(jnp.float32)[None],
    )


def contract_rows(left, right):
    return lax.dot_general(
        left, right, (((0,), (0,)), ((), ())), preferred_element_type=jnp.float32
    )


def solution(mesh):
    placed = (
        P("pipe", "tensor", None),
        P("pipe", "tensor", None),
        P("pipe", "tensor", None),
        P("pipe", "tensor", None),
        P("pipe", "tensor", None),
        P("pipe", "tensor", None),
        P(None, "tensor", None),
        P(None, "pipe", None),
        P("pipe", None, None, "tensor"),
        P("pipe", None, "tensor", None),
    )
    return jax.shard_map(
        local,
        mesh=mesh,
        in_specs=placed,
        out_specs=(
            P("pipe", "tensor", None),
            P("pipe", "tensor", None),
            P("pipe", "tensor", None),
            P("pipe", "tensor", None),
            P("pipe", None, "tensor"),
            P("pipe", "tensor", None),
        ),
        check_vma=False,
    )
```

time: 341 us -> 273 us (0.80)
  the two profiles are of different devices: /device:TPU:96 before, /device:TPU:1 now
where the time goes in v1:
time: 273 us; the launch traced here: 272 us
  starting transfers between devices  97.5 us (36%)
  waiting for transfers between devices  92.3 us (34%)
  other arithmetic  33.5 us (12%)
  local copies, waits for them, and re-layouts  28.4 us (10%)
  matrix products  19 us (7%)
    ppermute x19, starting transfers between devices, moved(): return lax.ppermute(shard, ('pipe', 'tensor'), pairs)  66.5 us
    ppermute x19, waiting for transfers between devices, moved(): return lax.ppermute(shard, ('pipe', 'tensor'), pairs)  63.6 us
    all_to_all x7, starting transfers between devices, turned(): lax.all_to_all(blocks, 'tensor', split_axis=0, concat_axis=0, axis_index_...  31 us
    all_to_all x7, waiting for transfers between devices, turned(): lax.all_to_all(blocks, 'tensor', split_axis=0, concat_axis=0, axis_index_...  28.7 us
    dot_general x7, matrix products, product(): return jnp.einsum(spec, left, right, preferred_element_type=jnp.float32)  15.9 us
    unnamed x71, local copies, waits for them, and re-layouts  10.5 us
  transfers between devices with their start and end apart: 26, of which 11 were waited for; matrix products, arithmetic and copies ran while one was open for 19% of the time, Pallas kernels for 0%

profile of v1, /device:TPU:1, one launch (start us, length us, event | category | flops | bytes accessed | tf_op | source)
XLA Modules:
  0.0 272.0 jit_solution(14882647696909502155)
XLA Ops:
  0.6 1.6 select_bitcast_fusion
  3.1 3.1 %collective-permute-start.1 = (bf16[64,4096]{1,0:T(8,128)(2,1)}, bf16[64,4096]{1,0:T(8,128)(2,1)}, u32[]{:S(2)}, u32[]{:S(2)}) collective-permute-start(bf16[64,4096]{1,0:T(8,128)(2,1)} %pad_maximum_fusion.5), channel_id=1, source_target_pairs={{0,248},{1,249},{2,250},{3,251},{4,252},{5,253},{6,254},{7,255},{8... | collective-permute-start | bytes 1572872 | tf_op jit(solution)/shard_map/ppermute | solution.py:25
  8.4 3.7 %all-to-all-start = ((bf16[4,64,1024]{2,1,0:T(8,128)(2,1)}), bf16[4,64,1024]{2,1,0:T(8,128)(2,1)S(1)}, u32[]{:S(2)}, u32[]{:S(2)}) async-start(bf16[4,64,1024]{2,1,0:T(8,128)(2,1)} %maximum_bitcast_fusion.4), calls=%async_computation | async-start | bytes 1048576 | tf_op jit(solution)/shard_map/all_to_all | solution.py:49
  12.3 1.2 reshape.331
  13.5 1.2 reshape.333
  16.1 1.2 fusion.25
  17.3 1.1 fusion.22
  25.1 4.4 %all-to-all-start.1 = ((bf16[4,256,1024]{2,1,0:T(8,128)(2,1)}), bf16[4,256,1024]{2,1,0:T(8,128)(2,1)S(1)}, u32[]{:S(2)}, u32[]{:S(2)}) async-start(bf16[4,256,1024]{2,1,0:T(8,128)(2,1)} %bitcast.11), calls=%async_computation.1 | async-start | bytes 4194304 | tf_op jit(solution)/shard_map/all_to_all | solution.py:49
  29.4 6.7 %collective-permute-start.6 = (s32[4,256]{1,0:T(4,128)S(1)}, s32[4,256]{1,0:T(4,128)S(1)}, u32[]{:S(2)}, u32[]{:S(2)}) collective-permute-start(s32[4,256]{1,0:T(4,128)S(1)} %bitcast.204), channel_id=1, source_target_pairs={{0,248},{1,249},{2,250},{3,251},{4,252},{5,253},{6,254},{7,255},{8... | collective-permute-start | bytes 12296 | tf_op jit(solution)/shard_map/ppermute | solution.py:25
  36.9 4.0 %collective-permute-start.2 = (bf16[4,32,1024]{2,1,0:T(8,128)(2,1)}, bf16[4,32,1024]{2,1,0:T(8,128)(2,1)S(1)}, u32[]{:S(2)}, u32[]{:S(2)}) collective-permute-start(bf16[4,32,1024]{2,1,0:T(8,128)(2,1)} %get-tuple-element.60), channel_id=1, source_target_pairs={{0,248},{1,249},{2,250},{3,251},{4,252},{5,253},{6,254},{7,255},{8... | collective-permute-start | bytes 786440 | tf_op jit(solution)/shard_map/ppermute | solution.py:25
  40.8 6.4 %collective-permute-start.3 = (bf16[4,32,1024]{2,1,0:T(8,128)(2,1)}, bf16[4,32,1024]{2,1,0:T(8,128)(2,1)}, u32[]{:S(2)}, u32[]{:S(2)}) collective-permute-start(bf16[4,32,1024]{2,1,0:T(8,128)(2,1)} %get-tuple-element.60), channel_id=1, source_target_pairs={{0,249},{1,248},{2,251},{3,250},{4,253},{5,252},{6,255},{7,254},{8... | collective-permute-start | bytes 786440 | tf_op jit(solution)/shard_map/ppermute | solution.py:25
  47.2 1.9 collective-permute-start.4
  49.1 3.9 %collective-permute-start.5 = (bf16[4,32,1024]{2,1,0:T(8,128)(2,1)S(1)}, bf16[4,32,1024]{2,1,0:T(8,128)(2,1)}, u32[]{:S(2)}, u32[]{:S(2)}) collective-permute-start(bf16[4,32,1024]{2,1,0:T(8,128)(2,1)S(1)} %get-tuple-element.61), channel_id=1, source_target_pairs={{0,241},{1,240},{2,243},{3,242},{4,245},{5,244},{6,247},{7,246},{8... | collective-permute-start | bytes 786440 | tf_op jit(solution)/shard_map/ppermute | solution.py:25
  53.1 2.3 slice.171
  55.4 2.3 copy.97
  57.7 6.5 %collective-permute-done.3 = bf16[4,32,1024]{2,1,0:T(8,128)(2,1)} collective-permute-done((bf16[4,32,1024]{2,1,0:T(8,128)(2,1)}, bf16[4,32,1024]{2,1,0:T(8,128)(2,1)}, u32[]{:S(2)}, u32[]{:S(2)}) %collective-permute-start.3) | collective-permute-done | bytes 262176 | tf_op jit(solution)/shard_map/ppermute | solution.py:25
  64.2 3.4 %collective-permute-done.4 = bf16[4,32,1024]{2,1,0:T(8,128)(2,1)} collective-permute-done((bf16[4,32,1024]{2,1,0:T(8,128)(2,1)S(1)}, bf16[4,32,1024]{2,1,0:T(8,128)(2,1)}, u32[]{:S(2)}, u32[]{:S(2)}) %collective-permute-start.4) | collective-permute-done | bytes 262176 | tf_op jit(solution)/shard_map/ppermute | solution.py:25
  67.6 1.9 fusion.2
  69.5 1.3 pad_maximum_fusion
  70.8 5.0 %all-to-all-start.2 = ((bf16[4,1536,128]{1,2,0:T(8,128)(2,1)}), bf16[4,1536,128]{1,2,0:T(8,128)(2,1)}, u32[]{:S(2)}, u32[]{:S(2)}) async-start(bf16[4,1536,128]{1,2,0:T(8,128)(2,1)} %pad_maximum_fusion), calls=%async_computation.2 | async-start | bytes 3145728 | tf_op jit(solution)/shard_map/all_to_all | solution.py:49
  78.5 3.9 %collective-permute-start.8 = (bf16[4,32,1024]{2,1,0:T(8,128)(2,1)}, bf16[4,32,1024]{2,1,0:T(8,128)(2,1)}, u32[]{:S(2)}, u32[]{:S(2)}) collective-permute-start(bf16[4,32,1024]{2,1,0:T(8,128)(2,1)} %get-tuple-element.46), channel_id=1, source_target_pairs={{0,248},{1,249},{2,250},{3,251},{4,252},{5,253},{6,254},{7,255},{8... | collective-permute-start | bytes 786440 | tf_op jit(solution)/shard_map/ppermute | solution.py:25
  82.5 3.7 %collective-permute-start.9 = (bf16[4,32,1024]{2,1,0:T(8,128)(2,1)}, bf16[4,32,1024]{2,1,0:T(8,128)(2,1)}, u32[]{:S(2)}, u32[]{:S(2)}) collective-permute-start(bf16[4,32,1024]{2,1,0:T(8,128)(2,1)} %get-tuple-element.46), channel_id=1, source_target_pairs={{0,249},{1,248},{2,251},{3,250},{4,253},{5,252},{6,255},{7,254},{8... | collective-permute-start | bytes 786440 | tf_op jit(solution)/shard_map/ppermute | solution.py:25
  86.2 3.0 %collective-permute-start.7 = (bf16[4,32,1024]{2,1,0:T(8,128)(2,1)}, bf16[4,32,1024]{2,1,0:T(8,128)(2,1)}, u32[]{:S(2)}, u32[]{:S(2)}) collective-permute-start(bf16[4,32,1024]{2,1,0:T(8,128)(2,1)} %get-tuple-element.47), channel_id=1, source_target_pairs={{0,1},{1,0},{2,3},{3,2},{4,5},{5,4},{6,7},{7,6},{8,9},{9,8},{10,11... | collective-permute-start | bytes 786440 | tf_op jit(solution)/shard_map/ppermute | solution.py:25
  89.2 6.3 %all-to-all-done.2 = bf16[4,1536,128]{1,2,0:T(8,128)(2,1)} async-done(((bf16[4,1536,128]{1,2,0:T(8,128)(2,1)}), bf16[4,1536,128]{1,2,0:T(8,128)(2,1)}, u32[]{:S(2)}, u32[]{:S(2)}) %all-to-all-start.2) | async-done | bytes 1572896 | tf_op jit(solution)/shard_map/all_to_all | solution.py:49
  95.5 1.1 convert_reduce_fusion
  99.1 5.9 %collective-permute-done.7 = bf16[4,32,1024]{2,1,0:T(8,128)(2,1)} collective-permute-done((bf16[4,32,1024]{2,1,0:T(8,128)(2,1)}, bf16[4,32,1024]{2,1,0:T(8,128)(2,1)}, u32[]{:S(2)}, u32[]{:S(2)}) %collective-permute-start.7) | collective-permute-done | bytes 262176 | tf_op jit(solution)/shard_map/ppermute | solution.py:25
  105.0 4.2 %collective-permute-done.9 = bf16[4,32,1024]{2,1,0:T(8,128)(2,1)} collective-permute-done((bf16[4,32,1024]{2,1,0:T(8,128)(2,1)}, bf16[4,32,1024]{2,1,0:T(8,128)(2,1)}, u32[]{:S(2)}, u32[]{:S(2)}) %collective-permute-start.9) | collective-permute-done | bytes 262176 | tf_op jit(solution)/shard_map/ppermute | solution.py:25
  109.1 2.2 fusion.3
  111.4 1.1 pad_maximum_fusion.2
  112.5 4.5 %all-to-all-start.3 = ((bf16[4,1024,128]{1,2,0:T(8,128)(2,1)}), bf16[4,1024,128]{1,2,0:T(8,128)(2,1)}, u32[]{:S(2)}, u32[]{:S(2)}) async-start(bf16[4,1024,128]{1,2,0:T(8,128)(2,1)} %pad_maximum_fusion.2), calls=%async_computation.3 | async-start | bytes 2097152 | tf_op jit(solution)/shard_map/all_to_all | solution.py:49
  117.1 3.9 %collective-permute-start.13 = (bf16[4,32,1024]{2,1,0:T(8,128)(2,1)S(1)}, bf16[4,32,1024]{2,1,0:T(8,128)(2,1)S(1)}, u32[]{:S(2)}, u32[]{:S(2)}) collective-permute-start(bf16[4,32,1024]{2,1,0:T(8,128)(2,1)S(1)} %get-tuple-element.44), channel_id=1, source_target_pairs={{0,1},{1,0},{2,3},{3,2},{4,5},{5,4},{6,7},{7,6},{8,9},{9,8},{10,11... | collective-permute-start | bytes 786440 | tf_op jit(solution)/shard_map/ppermute | solution.py:25
  121.0 5.4 %collective-permute-start.14 = (bf16[4,32,1024]{2,1,0:T(8,128)(2,1)S(1)}, bf16[4,32,1024]{2,1,0:T(8,128)(2,1)S(1)}, u32[]{:S(2)}, u32[]{:S(2)}) collective-permute-start(bf16[4,32,1024]{2,1,0:T(8,128)(2,1)S(1)} %get-tuple-element.45), channel_id=1, source_target_pairs={{0,248},{1,249},{2,250},{3,251},{4,252},{5,253},{6,254},{7,255},{8... | collective-permute-start | bytes 786440 | tf_op jit(solution)/shard_map/ppermute | solution.py:25
  126.4 12.6 %collective-permute-done.13 = bf16[4,32,1024]{2,1,0:T(8,128)(2,1)S(1)} collective-permute-done((bf16[4,32,1024]{2,1,0:T(8,128)(2,1)S(1)}, bf16[4,32,1024]{2,1,0:T(8,128)(2,1)S(1)}, u32[]{:S(2)}, u32[]{:S(2)}) %collective-permute-start.13) | collective-permute-done | bytes 262176 | tf_op jit(solution)/shard_map/ppermute | solution.py:25
  139.0 11.0 %collective-permute-done.14 = bf16[4,32,1024]{2,1,0:T(8,128)(2,1)S(1)} collective-permute-done((bf16[4,32,1024]{2,1,0:T(8,128)(2,1)S(1)}, bf16[4,32,1024]{2,1,0:T(8,128)(2,1)S(1)}, u32[]{:S(2)}, u32[]{:S(2)}) %collective-permute-start.14) | collective-permute-done | bytes 262176 | tf_op jit(solution)/shard_map/ppermute | solution.py:25
  150.8 2.1 fusion.4
  152.8 1.1 slice_reduce_fusion.1
  154.7 1.1 pad_maximum_fusion.3
  155.8 4.4 %all-to-all-start.4 = ((bf16[4,1024,128]{1,2,0:T(8,128)(2,1)}), bf16[4,1024,128]{1,2,0:T(8,128)(2,1)}, u32[]{:S(2)}, u32[]{:S(2)}) async-start(bf16[4,1024,128]{1,2,0:T(8,128)(2,1)} %pad_maximum_fusion.3), calls=%async_computation.4 | async-start | bytes 2097152 | tf_op jit(solution)/shard_map/all_to_all | solution.py:49
  160.3 2.2 bitcast_convert_fusion.1
  162.5 3.9 %collective-permute-start.10 = (bf16[4,32,1024]{2,1,0:T(8,128)(2,1)S(1)}, bf16[4,32,1024]{2,1,0:T(8,128)(2,1)S(1)}, u32[]{:S(2)}, u32[]{:S(2)}) collective-permute-start(bf16[4,32,1024]{2,1,0:T(8,128)(2,1)S(1)} %fusion.61), channel_id=1, source_target_pairs={{0,1},{1,0},{2,3},{3,2},{4,5},{5,4},{6,7},{7,6},{8,9},{9,8},{10,11... | collective-permute-start | bytes 786440 | tf_op jit(solution)/shard_map/ppermute | solution.py:25
  167.2 4.2 %collective-permute-start.12 = (bf16[4,32,1024]{2,1,0:T(8,128)(2,1)}, bf16[4,32,1024]{2,1,0:T(8,128)(2,1)S(1)}, u32[]{:S(2)}, u32[]{:S(2)}) collective-permute-start(bf16[4,32,1024]{2,1,0:T(8,128)(2,1)} %bitcast.32), channel_id=1, source_target_pairs={{0,249},{1,248},{2,251},{3,250},{4,253},{5,252},{6,255},{7,254},{8... | collective-permute-start | bytes 786440 | tf_op jit(solution)/shard_map/ppermute | solution.py:25
  171.5 2.8 %fusion.1 = bf16[4,1024,128]{1,2,0:T(8,128)(2,1)} fusion(bf16[4,1024,128]{1,2,0:T(8,128)(2,1)} %all-to-all-done.3, bf16[128,1024]{1,0:T(8,128)(2,1)S(1)} %bitcast.212, bf16[128,1024]{1,0:T(8,128)(2,1)S(1)} %bitcast.210, bf16[128,1024]{1,0:T(8,128)(2,1)S(1)} %bitcast.208, bf16[128,1024]{1,0:T(8,128)(2,1)S(1)} %bitcast.199), kind=kOutput, calls=%fused_computation.9 | convolution fusion | flops 541589504 | bytes 2621440 | tf_op jit(solution)/shard_map/rd,hrk->hdk/dot_general | solution.py:84
  174.2 1.9 collective-permute-done.10
  176.9 1.1 slice_reduce_fusion
  178.8 2.5 pad_maximum_fusion.1
  181.2 4.4 %all-to-all-start.5 = ((bf16[4,1536,128]{1,2,0:T(8,128)(2,1)}), bf16[4,1536,128]{1,2,0:T(8,128)(2,1)}, u32[]{:S(2)}, u32[]{:S(2)}) async-start(bf16[4,1536,128]{1,2,0:T(8,128)(2,1)} %pad_maximum_fusion.1), calls=%async_computation.5 | async-start | bytes 3145728 | tf_op jit(solution)/shard_map/all_to_all | solution.py:49
  185.6 1.8 bitcast_convert_fusion
  187.4 6.1 %collective-permute-start.16 = (bf16[4,32,1024]{2,1,0:T(8,128)(2,1)S(1)}, bf16[4,32,1024]{2,1,0:T(8,128)(2,1)S(1)}, u32[]{:S(2)}, u32[]{:S(2)}) collective-permute-start(bf16[4,32,1024]{2,1,0:T(8,128)(2,1)S(1)} %fusion.63), channel_id=1, source_target_pairs={{0,1},{1,0},{2,3},{3,2},{4,5},{5,4},{6,7},{7,6},{8,9},{9,8},{10,11... | collective-permute-start | bytes 786440 | tf_op jit(solution)/shard_map/ppermute | solution.py:25
  193.5 6.4 %collective-permute-start.17 = (bf16[4,32,1024]{2,1,0:T(8,128)(2,1)S(1)}, bf16[4,32,1024]{2,1,0:T(8,128)(2,1)S(1)}, u32[]{:S(2)}, u32[]{:S(2)}) collective-permute-start(bf16[4,32,1024]{2,1,0:T(8,128)(2,1)S(1)} %bitcast.197), channel_id=1, source_target_pairs={{0,248},{1,249},{2,250},{3,251},{4,252},{5,253},{6,254},{7,255},{8... | collective-permute-start | bytes 786440 | tf_op jit(solution)/shard_map/ppermute | solution.py:25
  200.7 6.6 %collective-permute-done.16 = bf16[4,32,1024]{2,1,0:T(8,128)(2,1)S(1)} collective-permute-done((bf16[4,32,1024]{2,1,0:T(8,128)(2,1)S(1)}, bf16[4,32,1024]{2,1,0:T(8,128)(2,1)S(1)}, u32[]{:S(2)}, u32[]{:S(2)}) %collective-permute-start.16) | collective-permute-done | bytes 262176 | tf_op jit(solution)/shard_map/ppermute | solution.py:25
  208.0 11.6 %collective-permute-done.17 = bf16[4,32,1024]{2,1,0:T(8,128)(2,1)S(1)} collective-permute-done((bf16[4,32,1024]{2,1,0:T(8,128)(2,1)S(1)}, bf16[4,32,1024]{2,1,0:T(8,128)(2,1)S(1)}, u32[]{:S(2)}, u32[]{:S(2)}) %collective-permute-start.17) | collective-permute-done | bytes 262176 | tf_op jit(solution)/shard_map/ppermute | solution.py:25
  220.5 3.0 %fusion = bf16[4,256,1024]{2,1,0:T(8,128)(2,1)} fusion(bf16[4,256,1024]{2,1,0:T(8,128)(2,1)} %fusion.55, bf16[4,1536,128]{1,2,0:T(8,128)(2,1)} %all-to-all-done.5, bf16[128,1024]{1,0:T(8,128)(2,1)} %bitcast.16, bf16[128,1024]{1,0:T(8,128)(2,1)} %bitcast.15, bf16[128,1024]{1,0:T(8,128)(2,1)} %bitcast.14, bf16[128,1024]{1,0:T(8,128)(2,1)S(1)} %bitcast.206), kind=kOutput, calls=%fused_computation.7 | convolution fusion | flops 541589504 | bytes 2621440 | tf_op jit(solution)/shard_map/hrk,rd->hkd/dot_general | solution.py:84
  223.4 4.7 %all-to-all-start.6 = ((bf16[4,256,1024]{2,1,0:T(8,128)(2,1)}), bf16[4,256,1024]{2,1,0:T(8,128)(2,1)}, u32[]{:S(2)}, u32[]{:S(2)}) async-start(bf16[4,256,1024]{2,1,0:T(8,128)(2,1)} %fusion), calls=%async_computation.6 | async-start | bytes 4194304 | tf_op jit(solution)/shard_map/all_to_all | solution.py:49
  229.0 1.5 slice_convert_fusion
  230.4 1.8 copy.115
  232.3 22.4 %all-to-all-done.6 = bf16[4,256,1024]{2,1,0:T(8,128)(2,1)} async-done(((bf16[4,256,1024]{2,1,0:T(8,128)(2,1)}), bf16[4,256,1024]{2,1,0:T(8,128)(2,1)}, u32[]{:S(2)}, u32[]{:S(2)}) %all-to-all-start.6) | async-done | bytes 2097184 | tf_op jit(solution)/shard_map/all_to_all | solution.py:49
  254.7 1.8 convert_bitcast_fusion.1
  259.0 1.1 copy.131
  260.4 1.1 copy.129
  261.9 1.1 copy.132
  263.0 1.9 copy.116
  264.9 2.9 %copy.117 = f32[1,128,4096]{2,1,0:T(8,128)} copy(f32[1,128,4096]{1,2,0:T(8,128)} %bitcast.173) | data formatting | bytes 4194304
  267.8 2.1 fusion.58
  269.9 2.0 fusion.59
  (165 shorter events, 27.5 us)
Async XLA Ops:
  3.1 13.0 %collective-permute-start.1 = (bf16[64,4096]{1,0:T(8,128)(2,1)}, bf16[64,4096]{1,0:T(8,128)(2,1)}, u32[]{:S(2)}, u32[]{:S(2)}) collective-permute-start(bf16[64,4096]{1,0:T(8,128)(2,1)} %pad_maximum_fusion.5), channel_id=1, source_target_pairs={{0,248},{1,249},{2,250},{3,251},{4,252},{5,253},{6,254},{7,255},{8... | collective-permute-start | bytes 1572872 | tf_op jit(solution)/shard_map/ppermute | solution.py:25
  7.0 5.1 %copy-start = (bf16[1,32,4096]{2,1,0:T(8,128)(2,1)S(1)}, bf16[1,32,4096]{2,1,0:T(8,128)(2,1)}, u32[]{:S(2)}) copy-start(bf16[1,32,4096]{2,1,0:T(8,128)(2,1)} %param.12) | copy-start | bytes 786436
  7.0 10.3 %collective-permute-start = (bf16[64,4096]{1,0:T(8,128)(2,1)}, bf16[64,4096]{1,0:T(8,128)(2,1)}, u32[]{:S(2)}, u32[]{:S(2)}) collective-permute-start(bf16[64,4096]{1,0:T(8,128)(2,1)} %pad_maximum_fusion.4), channel_id=1, source_target_pairs={{0,8},{1,9},{2,10},{3,11},{4,12},{5,13},{6,14},{7,15},{8,16},{9,17... | collective-permute-start | bytes 1572872 | tf_op jit(solution)/shard_map/ppermute | solution.py:25
  7.4 6.1 %copy-start.1 = (bf16[1,32,4096]{2,1,0:T(8,128)(2,1)S(1)}, bf16[1,32,4096]{2,1,0:T(8,128)(2,1)}, u32[]{:S(2)}) copy-start(bf16[1,32,4096]{2,1,0:T(8,128)(2,1)} %param.13) | copy-start | bytes 786436
  8.4 16.6 %all-to-all-start = ((bf16[4,64,1024]{2,1,0:T(8,128)(2,1)}), bf16[4,64,1024]{2,1,0:T(8,128)(2,1)S(1)}, u32[]{:S(2)}, u32[]{:S(2)}) async-start(bf16[4,64,1024]{2,1,0:T(8,128)(2,1)} %maximum_bitcast_fusion.4), calls=%async_computation | async-start | bytes 1048576 | tf_op jit(solution)/shard_map/all_to_all | solution.py:49
  12.1 2.5 slice-start
  15.9 6.2 %copy-start.5 = (f32[32,4,1024]{2,1,0:T(4,128)S(1)}, f32[32,4,1024]{2,1,0:T(4,128)}, u32[]{:S(2)}) copy-start(f32[32,4,1024]{2,1,0:T(4,128)} %reshape.331) | copy-start | bytes 1572868
  15.9 7.2 %copy-start.4 = (f32[32,4,1024]{2,1,0:T(4,128)S(1)}, f32[32,4,1024]{2,1,0:T(4,128)}, u32[]{:S(2)}) copy-start(f32[32,4,1024]{2,1,0:T(4,128)} %reshape.333) | copy-start | bytes 1572868
  16.0 7.0 %copy-start.16 = (f32[32]{0:T(128)}, f32[32]{0:T(128)S(1)}, u32[]{:S(2)}) copy-start(f32[32]{0:T(128)S(1)} %add_rsqrt_fusion.1) | copy-start | bytes 388
  16.1 6.9 %copy-start.14 = (f32[32]{0:T(128)}, f32[32]{0:T(128)S(1)}, u32[]{:S(2)}) copy-start(f32[32]{0:T(128)S(1)} %add_rsqrt_fusion) | copy-start | bytes 388
  25.1 4.4 %copy-start.13 = (s32[4,1,256]{2,1,0:T(1,128)S(1)}, s32[4,1,256]{2,1,0:T(1,128)}, u32[]{:S(2)}) copy-start(s32[4,1,256]{2,1,0:T(1,128)} %param.17) | copy-start | bytes 12292
  25.1 42.5 %all-to-all-start.1 = ((bf16[4,256,1024]{2,1,0:T(8,128)(2,1)}), bf16[4,256,1024]{2,1,0:T(8,128)(2,1)S(1)}, u32[]{:S(2)}, u32[]{:S(2)}) async-start(bf16[4,256,1024]{2,1,0:T(8,128)(2,1)} %bitcast.11), calls=%async_computation.1 | async-start | bytes 4194304 | tf_op jit(solution)/shard_map/all_to_all | solution.py:49
  29.4 46.7 %collective-permute-start.6 = (s32[4,256]{1,0:T(4,128)S(1)}, s32[4,256]{1,0:T(4,128)S(1)}, u32[]{:S(2)}, u32[]{:S(2)}) collective-permute-start(s32[4,256]{1,0:T(4,128)S(1)} %bitcast.204), channel_id=1, source_target_pairs={{0,248},{1,249},{2,250},{3,251},{4,252},{5,253},{6,254},{7,255},{8... | collective-permute-start | bytes 12296 | tf_op jit(solution)/shard_map/ppermute | solution.py:25
  36.9 20.9 %collective-permute-start.2 = (bf16[4,32,1024]{2,1,0:T(8,128)(2,1)}, bf16[4,32,1024]{2,1,0:T(8,128)(2,1)S(1)}, u32[]{:S(2)}, u32[]{:S(2)}) collective-permute-start(bf16[4,32,1024]{2,1,0:T(8,128)(2,1)} %get-tuple-element.60), channel_id=1, source_target_pairs={{0,248},{1,249},{2,250},{3,251},{4,252},{5,253},{6,254},{7,255},{8... | collective-permute-start | bytes 786440 | tf_op jit(solution)/shard_map/ppermute | solution.py:25
  40.8 23.4 %collective-permute-start.3 = (bf16[4,32,1024]{2,1,0:T(8,128)(2,1)}, bf16[4,32,1024]{2,1,0:T(8,128)(2,1)}, u32[]{:S(2)}, u32[]{:S(2)}) collective-permute-start(bf16[4,32,1024]{2,1,0:T(8,128)(2,1)} %get-tuple-element.60), channel_id=1, source_target_pairs={{0,249},{1,248},{2,251},{3,250},{4,253},{5,252},{6,255},{7,254},{8... | collective-permute-start | bytes 786440 | tf_op jit(solution)/shard_map/ppermute | solution.py:25
  47.2 20.3 %collective-permute-start.4 = (bf16[4,32,1024]{2,1,0:T(8,128)(2,1)S(1)}, bf16[4,32,1024]{2,1,0:T(8,128)(2,1)}, u32[]{:S(2)}, u32[]{:S(2)}) collective-permute-start(bf16[4,32,1024]{2,1,0:T(8,128)(2,1)S(1)} %get-tuple-element.61), channel_id=1, source_target_pairs={{0,240},{1,241},{2,242},{3,243},{4,244},{5,245},{6,246},{7,247},{8... | collective-permute-start | bytes 786440 | tf_op jit(solution)/shard_map/ppermute | solution.py:25
  49.1 18.4 %collective-permute-start.5 = (bf16[4,32,1024]{2,1,0:T(8,128)(2,1)S(1)}, bf16[4,32,1024]{2,1,0:T(8,128)(2,1)}, u32[]{:S(2)}, u32[]{:S(2)}) collective-permute-start(bf16[4,32,1024]{2,1,0:T(8,128)(2,1)S(1)} %get-tuple-element.61), channel_id=1, source_target_pairs={{0,241},{1,240},{2,243},{3,242},{4,245},{5,244},{6,247},{7,246},{8... | collective-permute-start | bytes 786440 | tf_op jit(solution)/shard_map/ppermute | solution.py:25
  57.7 11.8 %copy-start.22 = (bf16[4,32,1024]{2,1,0:T(8,128)(2,1)}, bf16[4,32,1024]{2,1,0:T(8,128)(2,1)S(1)}, u32[]{:S(2)}) copy-start(bf16[4,32,1024]{2,1,0:T(8,128)(2,1)S(1)} %collective-permute-done.2) | copy-start | bytes 786436
  67.6 2.0 copy-start.2
  70.8 24.7 %all-to-all-start.2 = ((bf16[4,1536,128]{1,2,0:T(8,128)(2,1)}), bf16[4,1536,128]{1,2,0:T(8,128)(2,1)}, u32[]{:S(2)}, u32[]{:S(2)}) async-start(bf16[4,1536,128]{1,2,0:T(8,128)(2,1)} %pad_maximum_fusion), calls=%async_computation.2 | async-start | bytes 3145728 | tf_op jit(solution)/shard_map/all_to_all | solution.py:49
  76.6 18.9 %copy-start.11 = (s32[256]{0:T(256)}, s32[256]{0:T(256)S(1)}, u32[]{:S(2)}) copy-start(s32[256]{0:T(256)S(1)} %eq.89) | copy-start | bytes 3076
  78.5 38.5 %copy-start.9 = (bf16[4,32,1024]{2,1,0:T(8,128)(2,1)}, bf16[4,32,1024]{2,1,0:T(8,128)(2,1)S(1)}, u32[]{:S(2)}) copy-start(bf16[4,32,1024]{2,1,0:T(8,128)(2,1)S(1)} %get-tuple-element.44) | copy-start | bytes 786436
  78.5 26.4 %collective-permute-start.8 = (bf16[4,32,1024]{2,1,0:T(8,128)(2,1)}, bf16[4,32,1024]{2,1,0:T(8,128)(2,1)}, u32[]{:S(2)}, u32[]{:S(2)}) collective-permute-start(bf16[4,32,1024]{2,1,0:T(8,128)(2,1)} %get-tuple-element.46), channel_id=1, source_target_pairs={{0,248},{1,249},{2,250},{3,251},{4,252},{5,253},{6,254},{7,255},{8... | collective-permute-start | bytes 786440 | tf_op jit(solution)/shard_map/ppermute | solution.py:25
  82.5 26.7 %collective-permute-start.9 = (bf16[4,32,1024]{2,1,0:T(8,128)(2,1)}, bf16[4,32,1024]{2,1,0:T(8,128)(2,1)}, u32[]{:S(2)}, u32[]{:S(2)}) collective-permute-start(bf16[4,32,1024]{2,1,0:T(8,128)(2,1)} %get-tuple-element.46), channel_id=1, source_target_pairs={{0,249},{1,248},{2,251},{3,250},{4,253},{5,252},{6,255},{7,254},{8... | collective-permute-start | bytes 786440 | tf_op jit(solution)/shard_map/ppermute | solution.py:25
  86.2 18.8 %collective-permute-start.7 = (bf16[4,32,1024]{2,1,0:T(8,128)(2,1)}, bf16[4,32,1024]{2,1,0:T(8,128)(2,1)}, u32[]{:S(2)}, u32[]{:S(2)}) collective-permute-start(bf16[4,32,1024]{2,1,0:T(8,128)(2,1)} %get-tuple-element.47), channel_id=1, source_target_pairs={{0,1},{1,0},{2,3},{3,2},{4,5},{5,4},{6,7},{7,6},{8,9},{9,8},{10,11... | collective-permute-start | bytes 786440 | tf_op jit(solution)/shard_map/ppermute | solution.py:25
  112.5 40.3 %all-to-all-start.3 = ((bf16[4,1024,128]{1,2,0:T(8,128)(2,1)}), bf16[4,1024,128]{1,2,0:T(8,128)(2,1)}, u32[]{:S(2)}, u32[]{:S(2)}) async-start(bf16[4,1024,128]{1,2,0:T(8,128)(2,1)} %pad_maximum_fusion.2), calls=%async_computation.3 | async-start | bytes 2097152 | tf_op jit(solution)/shard_map/all_to_all | solution.py:49
  117.1 22.0 %collective-permute-start.13 = (bf16[4,32,1024]{2,1,0:T(8,128)(2,1)S(1)}, bf16[4,32,1024]{2,1,0:T(8,128)(2,1)S(1)}, u32[]{:S(2)}, u32[]{:S(2)}) collective-permute-start(bf16[4,32,1024]{2,1,0:T(8,128)(2,1)S(1)} %get-tuple-element.44), channel_id=1, source_target_pairs={{0,1},{1,0},{2,3},{3,2},{4,5},{5,4},{6,7},{7,6},{8,9},{9,8},{10,11... | collective-permute-start | bytes 786440 | tf_op jit(solution)/shard_map/ppermute | solution.py:25
  121.0 29.0 %collective-permute-start.14 = (bf16[4,32,1024]{2,1,0:T(8,128)(2,1)S(1)}, bf16[4,32,1024]{2,1,0:T(8,128)(2,1)S(1)}, u32[]{:S(2)}, u32[]{:S(2)}) collective-permute-start(bf16[4,32,1024]{2,1,0:T(8,128)(2,1)S(1)} %get-tuple-element.45), channel_id=1, source_target_pairs={{0,248},{1,249},{2,250},{3,251},{4,252},{5,253},{6,254},{7,255},{8... | collective-permute-start | bytes 786440 | tf_op jit(solution)/shard_map/ppermute | solution.py:25
  126.4 23.6 %collective-permute-start.15 = (bf16[4,32,1024]{2,1,0:T(8,128)(2,1)S(1)}, bf16[4,32,1024]{2,1,0:T(8,128)(2,1)S(1)}, u32[]{:S(2)}, u32[]{:S(2)}) collective-permute-start(bf16[4,32,1024]{2,1,0:T(8,128)(2,1)S(1)} %get-tuple-element.45), channel_id=1, source_target_pairs={{0,249},{1,248},{2,251},{3,250},{4,253},{5,252},{6,255},{7,254},{8... | collective-permute-start | bytes 786440 | tf_op jit(solution)/shard_map/ppermute | solution.py:25
  139.0 11.0 %copy-start.24 = (bf16[4,32,1024]{2,1,0:T(8,128)(2,1)}, bf16[4,32,1024]{2,1,0:T(8,128)(2,1)S(1)}, u32[]{:S(2)}) copy-start(bf16[4,32,1024]{2,1,0:T(8,128)(2,1)S(1)} %collective-permute-done.13) | copy-start | bytes 786436
  150.0 0.7 copy-start.26
  150.0 0.8 copy-start.28
  150.8 3.2 %copy-start.12 = (s32[256]{0:T(256)S(1)}, s32[256]{0:T(256)}, u32[]{:S(2)}) copy-start(s32[256]{0:T(256)} %copy-done.11) | copy-start | bytes 3076
  150.8 3.2 %copy-start.21 = (f32[256]{0:T(256)S(1)}, f32[256]{0:T(256)}, u32[]{:S(2)}) copy-start(f32[256]{0:T(256)} %get-tuple-element.34) | copy-start | bytes 3076
  150.8 3.5 %copy-start.20 = (f32[256]{0:T(256)S(1)}, f32[256]{0:T(256)}, u32[]{:S(2)}) copy-start(f32[256]{0:T(256)} %get-tuple-element.36) | copy-start | bytes 3076
  155.8 21.1 %all-to-all-start.4 = ((bf16[4,1024,128]{1,2,0:T(8,128)(2,1)}), bf16[4,1024,128]{1,2,0:T(8,128)(2,1)}, u32[]{:S(2)}, u32[]{:S(2)}) async-start(bf16[4,1024,128]{1,2,0:T(8,128)(2,1)} %pad_maximum_fusion.3), calls=%async_computation.4 | async-start | bytes 2097152 | tf_op jit(solution)/shard_map/all_to_all | solution.py:49
  160.2 11.2 %copy-start.10 = (bf16[4,32,1024]{2,1,0:T(8,128)(2,1)S(1)}, bf16[4,32,1024]{2,1,0:T(8,128)(2,1)}, u32[]{:S(2)}) copy-start(bf16[4,32,1024]{2,1,0:T(8,128)(2,1)} %copy-done.9) | copy-start | bytes 786436
  160.2 11.2 %copy-start.25 = (bf16[4,32,1024]{2,1,0:T(8,128)(2,1)S(1)}, bf16[4,32,1024]{2,1,0:T(8,128)(2,1)}, u32[]{:S(2)}) copy-start(bf16[4,32,1024]{2,1,0:T(8,128)(2,1)} %copy-done.24) | copy-start | bytes 786436
  160.2 11.2 %copy-start.27 = (bf16[4,32,1024]{2,1,0:T(8,128)(2,1)S(1)}, bf16[4,32,1024]{2,1,0:T(8,128)(2,1)}, u32[]{:S(2)}) copy-start(bf16[4,32,1024]{2,1,0:T(8,128)(2,1)} %copy-done.26) | copy-start | bytes 786436
  160.3 11.2 %copy-start.29 = (bf16[4,32,1024]{2,1,0:T(8,128)(2,1)S(1)}, bf16[4,32,1024]{2,1,0:T(8,128)(2,1)}, u32[]{:S(2)}) copy-start(bf16[4,32,1024]{2,1,0:T(8,128)(2,1)} %copy-done.28) | copy-start | bytes 786436
  162.5 13.7 %collective-permute-start.10 = (bf16[4,32,1024]{2,1,0:T(8,128)(2,1)S(1)}, bf16[4,32,1024]{2,1,0:T(8,128)(2,1)S(1)}, u32[]{:S(2)}, u32[]{:S(2)}) collective-permute-start(bf16[4,32,1024]{2,1,0:T(8,128)(2,1)S(1)} %fusion.61), channel_id=1, source_target_pairs={{0,1},{1,0},{2,3},{3,2},{4,5},{5,4},{6,7},{7,6},{8,9},{9,8},{10,11... | collective-permute-start | bytes 786440 | tf_op jit(solution)/shard_map/ppermute | solution.py:25
  167.2 32.7 %collective-permute-start.11 = (bf16[4,32,1024]{2,1,0:T(8,128)(2,1)}, bf16[4,32,1024]{2,1,0:T(8,128)(2,1)S(1)}, u32[]{:S(2)}, u32[]{:S(2)}) collective-permute-start(bf16[4,32,1024]{2,1,0:T(8,128)(2,1)} %bitcast.31), channel_id=1, source_target_pairs={{0,248},{1,249},{2,250},{3,251},{4,252},{5,253},{6,254},{7,255},{8... | collective-permute-start | bytes 786440 | tf_op jit(solution)/shard_map/ppermute | solution.py:25
  167.2 10.8 %copy-start.19 = (f32[256]{0:T(256)S(1)}, f32[256]{0:T(256)}, u32[]{:S(2)}) copy-start(f32[256]{0:T(256)} %get-tuple-element.37) | copy-start | bytes 3076
  167.2 32.7 %collective-permute-start.12 = (bf16[4,32,1024]{2,1,0:T(8,128)(2,1)}, bf16[4,32,1024]{2,1,0:T(8,128)(2,1)S(1)}, u32[]{:S(2)}, u32[]{:S(2)}) collective-permute-start(bf16[4,32,1024]{2,1,0:T(8,128)(2,1)} %bitcast.32), channel_id=1, source_target_pairs={{0,249},{1,248},{2,251},{3,250},{4,253},{5,252},{6,255},{7,254},{8... | collective-permute-start | bytes 786440 | tf_op jit(solution)/shard_map/ppermute | solution.py:25
  174.2 4.1 %copy-start.18 = (f32[256]{0:T(256)S(1)}, f32[256]{0:T(256)}, u32[]{:S(2)}) copy-start(f32[256]{0:T(256)} %get-tuple-element.35) | copy-start | bytes 3076
  181.2 39.2 %all-to-all-start.5 = ((bf16[4,1536,128]{1,2,0:T(8,128)(2,1)}), bf16[4,1536,128]{1,2,0:T(8,128)(2,1)}, u32[]{:S(2)}, u32[]{:S(2)}) async-start(bf16[4,1536,128]{1,2,0:T(8,128)(2,1)} %pad_maximum_fusion.1), calls=%async_computation.5 | async-start | bytes 3145728 | tf_op jit(solution)/shard_map/all_to_all | solution.py:49
  187.4 33.1 %copy-start.23 = (bf16[4,32,1024]{2,1,0:T(8,128)(2,1)S(1)}, bf16[4,32,1024]{2,1,0:T(8,128)(2,1)}, u32[]{:S(2)}) copy-start(bf16[4,32,1024]{2,1,0:T(8,128)(2,1)} %copy-done.22) | copy-start | bytes 786436
  187.4 19.8 %collective-permute-start.16 = (bf16[4,32,1024]{2,1,0:T(8,128)(2,1)S(1)}, bf16[4,32,1024]{2,1,0:T(8,128)(2,1)S(1)}, u32[]{:S(2)}, u32[]{:S(2)}) collective-permute-start(bf16[4,32,1024]{2,1,0:T(8,128)(2,1)S(1)} %fusion.63), channel_id=1, source_target_pairs={{0,1},{1,0},{2,3},{3,2},{4,5},{5,4},{6,7},{7,6},{8,9},{9,8},{10,11... | collective-permute-start | bytes 786440 | tf_op jit(solution)/shard_map/ppermute | solution.py:25
  193.5 26.1 %collective-permute-start.17 = (bf16[4,32,1024]{2,1,0:T(8,128)(2,1)S(1)}, bf16[4,32,1024]{2,1,0:T(8,128)(2,1)S(1)}, u32[]{:S(2)}, u32[]{:S(2)}) collective-permute-start(bf16[4,32,1024]{2,1,0:T(8,128)(2,1)S(1)} %bitcast.197), channel_id=1, source_target_pairs={{0,248},{1,249},{2,250},{3,251},{4,252},{5,253},{6,254},{7,255},{8... | collective-permute-start | bytes 786440 | tf_op jit(solution)/shard_map/ppermute | solution.py:25
  199.9 19.8 %collective-permute-start.18 = (bf16[4,32,1024]{2,1,0:T(8,128)(2,1)S(1)}, bf16[4,32,1024]{2,1,0:T(8,128)(2,1)S(1)}, u32[]{:S(2)}, u32[]{:S(2)}) collective-permute-start(bf16[4,32,1024]{2,1,0:T(8,128)(2,1)S(1)} %bitcast.196), channel_id=1, source_target_pairs={{0,249},{1,248},{2,251},{3,250},{4,253},{5,252},{6,255},{7,254},{8... | collective-permute-start | bytes 786440 | tf_op jit(solution)/shard_map/ppermute | solution.py:25
  223.4 31.3 %all-to-all-start.6 = ((bf16[4,256,1024]{2,1,0:T(8,128)(2,1)}), bf16[4,256,1024]{2,1,0:T(8,128)(2,1)}, u32[]{:S(2)}, u32[]{:S(2)}) async-start(bf16[4,256,1024]{2,1,0:T(8,128)(2,1)} %fusion), calls=%async_computation.6 | async-start | bytes 4194304 | tf_op jit(solution)/shard_map/all_to_all | solution.py:49
  256.5 1.0 copy-start.3
  256.6 1.0 copy-start.15
  256.6 1.0 copy-start.17
  264.9 2.9 %copy-start.7 = (f32[4,8,4,1024]{3,1,2,0:T(8,128)S(1)}, f32[4,8,4,1024]{3,1,2,0:T(8,128)}, u32[]{:S(2)}) copy-start(f32[4,8,4,1024]{3,1,2,0:T(8,128)} %copy.131) | copy-start | bytes 1572868
  267.8 2.1 copy-start.6
  267.8 2.1 copy-start.8
